TPU v7x, 32 devices: a whole 2x2x4 slice. The times are simulated.
32 devices in a mesh: dp: 4 (over y, x), row: 4 (over z), col: 2 (over core).
Axes of the slice: x: 2, y: 2, z: 4, core: 2. Of those that a mesh axis runs over, the one named last changes fastest.
Arguments:
- hidden_in: bfloat16 [32, 1024, 768], P(('dp', 'row'), None, 'col'), may hold values from -6 to 6
- encoded: bfloat16 [32, 256, 768], P(('dp', 'row'), None, 'col'), may hold values from -6 to 6
- cotangent: bfloat16 [32, 1024, 768], P(('dp', 'row'), None, 'col'), may hold values from -6 to 6
- piece_start: int32 [32, 2], P(('dp', 'row')), may hold values from 0 to 960, as said below
- image_piece_lengths: int32 [32, 2], P(('dp', 'row')), may hold values from 64 to 256, as said below
- bucket_table: int32 [2047], replicated, may hold values from 0 to 31
- self_query: bfloat16 [768, 768], P('row', 'col'), may hold values from -0.0546875 to 0.0546875
- self_key: bfloat16 [768, 768], P('row', 'col'), may hold values from -0.21875 to 0.21875
- self_value: bfloat16 [768, 768], P('row', 'col'), may hold values from -0.21875 to 0.21875
- self_out: bfloat16 [768, 768], P('col', 'row'), may hold values from -0.875 to 0.875
- rel_weight: bfloat16 [32, 12], P('row', 'col'), may hold values from -3 to 3
- cross_query: bfloat16 [768, 768], P('row', 'col'), may hold values from -0.0546875 to 0.0546875
- cross_key: bfloat16 [768, 768], P('row', 'col'), may hold values from -0.21875 to 0.21875
- cross_value: bfloat16 [768, 768], P('row', 'col'), may hold values from -0.21875 to 0.21875
- cross_out: bfloat16 [768, 768], P('col', 'row'), may hold values from -0.875 to 0.875
- ffn_gate: bfloat16 [768, 2048], P('row', 'col'), may hold values from -0.21875 to 0.21875
- ffn_up: bfloat16 [768, 2048], P('row', 'col'), may hold values from -0.21875 to 0.21875
- ffn_down: bfloat16 [2048, 768], P('col', 'row'), may hold values from -0.25 to 0.25
- gain_self: float32 [768], P('col'), may hold values from 0.25 to 1.75
- gain_cross: float32 [768], P('col'), may hold values from 0.25 to 1.75
- gain_ffn: float32 [768], P('col'), may hold values from 0.25 to 1.75
- gain_final: float32 [768], P('col'), may hold values from 0.25 to 1.75
Outputs:
- output: bfloat16 [32, 1024, 768], P(('dp', 'row'), None, 'col')
- hidden_grad: float32 [32, 1024, 768], P(('dp', 'row'), None, 'col')
- encoded_grad: float32 [32, 256, 768], P(('dp', 'row'), None, 'col')
- self_query_grad: float32 [768, 768], P('row', 'col')
- self_key_grad: float32 [768, 768], P('row', 'col')
- self_value_grad: float32 [768, 768], P('row', 'col')
- self_out_grad: float32 [768, 768], P('col', 'row')
- rel_weight_grad: float32 [32, 12], P('row', 'col')
- cross_query_grad: float32 [768, 768], P('row', 'col')
- cross_key_grad: float32 [768, 768], P('row', 'col')
- cross_value_grad: float32 [768, 768], P('row', 'col')
- cross_out_grad: float32 [768, 768], P('col', 'row')
- ffn_gate_grad: float32 [768, 2048], P('row', 'col')
- ffn_up_grad: float32 [768, 2048], P('row', 'col')
- ffn_down_grad: float32 [2048, 768], P('col', 'row')
- gain_self_grad: float32 [768], P('col')
- gain_cross_grad: float32 [768], P('col')
- gain_ffn_grad: float32 [768], P('col')
- gain_final_grad: float32 [768], P('col')
Inputs may be any that keep to these rules, and one draw needn't show every extreme that they name: `piece_start`: the p-th piece of a sequence lies inside positions p * 512 to (p + 1) * 512 - 1, so pieces never intersect. `image_piece_lengths`: some piece has exactly 256 tokens. `bucket_table`: entry j - i + 1023 is the bucket of a key at position j seen from a query at position i.
All inputs are finite; a program needn't handle non-finite values.
Results may differ from a plain program's by a relative error of at most 0.03.
The roundings to bfloat16 on the way count: a program that leaves them out, or rounds other values in their place, can miss the bound.
Values may be sent and summed in bfloat16 or wider, within the bound.
A program may use at most 256 MiB of HBM per device.

v0:
```python
import math

import jax
import jax.numpy as jnp
from jax import lax
from jax.experimental import pallas as pl
from jax.experimental.pallas import tpu as pltpu
from jax.sharding import PartitionSpec as P

D = 768
HALF = 384
L = 1024
LE = 256
BUCKETS = 32
SPAN = 1536
EPSILON = 1e-06
MASKED = -1e30
ROOT_TWO_PI = math.sqrt(2.0 / math.pi)
MESH = pl.DeviceIdType.MESH
ROWS = 4
QUAD = 4
BLOCK = D // ROWS
PIECE = BLOCK // QUAD
f32 = jnp.float32
bf16 = jnp.bfloat16
NT = (((1,), (1,)), ((), ()))
NN = (((1,), (0,)), ((), ()))
TN = (((0,), (0,)), ((), ()))
VMEM_LIMIT = 60 * 2**20


def dot(a, b, dims):
    return lax.dot_general(a, b, dims, preferred_element_type=f32)


def head_of(x, h):
    lane = lax.broadcasted_iota(jnp.int32, x.shape, 1)
    return jnp.where((lane >= 64 * h) & (lane < 64 * h + 64), x, jnp.zeros_like(x))


def transposed(x):
    return x.astype(f32).T.astype(bf16)


def spread_bias(t8_ref, table):
    for h in range(2):
        t = t8_ref[h]
        for m in range(16):
            table[h][8 * m : 8 * m + 8, :] = pltpu.roll(t, 8 * m, 1)


def allowed_rows(piece_ref, base, rows, width):
    s0 = piece_ref[0]
    s1 = piece_ref[1]
    e0 = piece_ref[2]
    e1 = piece_ref[3]
    c = lax.broadcasted_iota(jnp.int32, (1, width), 1) + base
    last = jnp.where(
        (c >= s0) & (c < e0), e0 - 1, jnp.where((c >= s1) & (c < e1), e1 - 1, 0)
    )
    last = jnp.maximum(c, last)
    return lax.broadcasted_iota(jnp.int32, (rows, width), 0) + base <= last


def extent(qb, width):
    return 512 * ((qb * width) // 512 + 1)


def biased_scores(k_ref, q_head, table, h, base, width, ext, ok):
    s = dot(k_ref[:ext, :], q_head, NT)
    bias = jnp.concatenate(
        [table[h][:, pl.ds(base - 128 * g + 512, width)] for g in range(ext // 128)], axis=0
    )
    s = s + bias
    tail = jnp.where(ok, s[base:], MASKED)
    return tail if base == 0 else jnp.concatenate([s[:base], tail], axis=0)


def softmax_cols(s):
    m = jnp.max(s, axis=0, keepdims=True)
    p = jnp.exp(s - m)
    total = jnp.sum(p, axis=0, keepdims=True)
    return (p.astype(bf16), total, m)


def tasks_of(width, group):
    tasks = [(qb, h) for qb in range(L // width) for h in range(2)]
    return [tasks[i : i + group] for i in range(0, len(tasks), group)]


def self_forward_body(piece_ref, q_ref, k_ref, v_ref, t8_ref, o_ref, lse_ref, table):
    width = 256
    vt = transposed(v_ref[...])
    spread_bias(t8_ref, table)
    oks = [
        allowed_rows(piece_ref, qb * width, extent(qb, width) - qb * width, width)
        for qb in range(L // width)
    ]
    outs = {}
    for group in tasks_of(width, 8):
        scored = [
            biased_scores(
                k_ref,
                head_of(q_ref[pl.ds(qb * width, width), :], h),
                table,
                h,
                qb * width,
                width,
                extent(qb, width),
                oks[qb],
            )
            for qb, h in group
        ]
        weights = [softmax_cols(s) for s in scored]
        for (qb, h), (p, total, m) in zip(group, weights):
            mixed = dot(vt[64 * h : 64 * h + 64, : extent(qb, width)], p, NN)
            outs[(qb, h)] = mixed * (1.0 / total)
            lse_ref[0, h : h + 1, pl.ds(qb * width, width)] = m + jnp.log(total)
            if h == 1:
                o_ref[pl.ds(qb * width, width), :] = (
                    jnp.concatenate([outs[(qb, 0)], outs[(qb, 1)]], axis=0).T.astype(bf16)
                )


def head_deltas(a_ref, da_ref):
    prod = (a_ref[...].astype(f32) * da_ref[...].astype(f32)).T
    return [jnp.sum(prod[64 * h : 64 * h + 64], axis=0, keepdims=True) for h in range(2)]


def self_backward_body(
    piece_ref,
    q_ref,
    k_ref,
    v_ref,
    t8_ref,
    a_ref,
    da_ref,
    lse_ref,
    dq_ref,
    dk_ref,
    dv_ref,
    diag_ref,
    table,
    spans,
    dk_sum,
    dv_sum,
):
    width = 256
    delta = head_deltas(a_ref, da_ref)
    kt = transposed(k_ref[...])
    spread_bias(t8_ref, table)
    for h in range(2):
        spans[h][...] = jnp.zeros(spans[h].shape, f32)
    dk_sum[...] = jnp.zeros_like(dk_sum)
    dv_sum[...] = jnp.zeros_like(dv_sum)
    for group in tasks_of(width, 2):
        qb = group[0][0]
        base = qb * width
        ext = extent(qb, width)
        ok = allowed_rows(piece_ref, base, ext - base, width)
        q = q_ref[pl.ds(base, width), :]
        da = da_ref[pl.ds(base, width), :]
        scored = [
            biased_scores(k_ref, head_of(q, h), table, h, base, width, ext, ok) for _, h in group
        ]
        dprobs = [dot(v_ref[:ext, :], head_of(da, h), NT) for _, h in group]
        low = []
        for h in range(2):
            p = jnp.exp(scored[h] - lse_ref[0, h : h + 1, pl.ds(base, width)])
            ds = p * (dprobs[h] - delta[h][:, base : base + width])
            for g in range(ext // 128):
                spans[h][:, pl.ds(base - 128 * g + 512, width)] += ds[128 * g : 128 * g + 128]
            low.append((p.astype(bf16), ds.astype(bf16)))
        dks = [dot(ds, q, NN) for _, ds in low]
        dvs = [dot(p, da, NN) for p, _ in low]
        dqs = [dot(kt[64 * h : 64 * h + 64, :ext], low[h][1], NN) for h in range(2)]
        lane = lax.broadcasted_iota(jnp.int32, (ext, 128), 1)
        dk_sum[:ext] += jnp.where(lane < 64, dks[0], dks[1])
        dv_sum[:ext] += jnp.where(lane < 64, dvs[0], dvs[1])
        dq_ref[pl.ds(base, width), :] = jnp.concatenate(dqs, axis=0).T.astype(bf16)
    dk_ref[...] = dk_sum[...].astype(bf16)
    dv_ref[...] = dv_sum[...].astype(bf16)
    for h in range(2):
        total = spans[h][0:8, :]
        for m in range(1, 16):
            total = total + pltpu.roll(spans[h][8 * m : 8 * m + 8, :], SPAN - 8 * m, 1)
        diag_ref[h] = total


def cross_forward_body(q_ref, k_ref, v_ref, o_ref, lse_ref):
    width = 256
    vt = transposed(v_ref[...])
    outs = {}
    for group in tasks_of(width, 8):
        scored = [
            dot(k_ref[...], head_of(q_ref[pl.ds(qb * width, width), :], h), NT) for qb, h in group
        ]
        weights = [softmax_cols(s) for s in scored]
        for (qb, h), (p, total, m) in zip(group, weights):
            outs[(qb, h)] = dot(vt[64 * h : 64 * h + 64, :], p, NN) * (1.0 / total)
            lse_ref[0, h : h + 1, pl.ds(qb * width, width)] = m + jnp.log(total)
            if h == 1:
                o_ref[pl.ds(qb * width, width), :] = (
                    jnp.concatenate([outs[(qb, 0)], outs[(qb, 1)]], axis=0).T.astype(bf16)
                )


def cross_backward_body(q_ref, k_ref, v_ref, a_ref, da_ref, lse_ref, dq_ref, dk_ref, dv_ref):
    width = 256
    delta = head_deltas(a_ref, da_ref)
    kt = transposed(k_ref[...])
    lane = lax.broadcasted_iota(jnp.int32, (LE, 128), 1)
    outs = {}
    dks = [None, None]
    dvs = [None, None]
    for group in tasks_of(width, 4):
        scored = [
            dot(k_ref[...], head_of(q_ref[pl.ds(qb * width, width), :], h), NT) for qb, h in group
        ]
        dprobs = [
            dot(v_ref[...], head_of(da_ref[pl.ds(qb * width, width), :], h), NT) for qb, h in group
        ]
        low = []
        for (qb, h), s, dp in zip(group, scored, dprobs):
            p = jnp.exp(s - lse_ref[0, h : h + 1, pl.ds(qb * width, width)])
            ds = p * (dp - delta[h][:, qb * width : (qb + 1) * width])
            low.append((p.astype(bf16), ds.astype(bf16)))
        for (qb, h), (p, ds) in zip(group, low):
            dk = dot(ds, q_ref[pl.ds(qb * width, width), :], NN)
            dv = dot(p, da_ref[pl.ds(qb * width, width), :], NN)
            dks[h] = dk if dks[h] is None else dks[h] + dk
            dvs[h] = dv if dvs[h] is None else dvs[h] + dv
            outs[(qb, h)] = dot(kt[64 * h : 64 * h + 64, :], ds, NN)
            if h == 1:
                dq_ref[pl.ds(qb * width, width), :] = (
                    jnp.concatenate([outs[(qb, 0)], outs[(qb, 1)]], axis=0).T.astype(bf16)
                )
    dk_ref[...] = jnp.where(lane < 64, dks[0], dks[1]).astype(bf16)
    dv_ref[...] = jnp.where(lane < 64, dvs[0], dvs[1]).astype(bf16)


def place():
    dp = lax.axis_index("dp")
    return (dp, dp % QUAD, lax.axis_index("row"), lax.axis_index("col"))


def quad_mate(dp, quarter, flip):
    return dp - quarter + (quarter ^ flip)


def greet_all(dp, quarter, row, col):
    barrier = pltpu.get_barrier_semaphore()
    for s in range(1, ROWS):
        pl.semaphore_signal(
            barrier, inc=1, device_id=(dp, (row + s) % ROWS, col), device_id_type=MESH
        )
    for k in range(1, QUAD):
        pl.semaphore_signal(
            barrier, inc=1, device_id=(quad_mate(dp, quarter, k), row, col), device_id_type=MESH
        )
    pl.semaphore_signal(barrier, inc=1, device_id=(dp, row, 1 - col), device_id_type=MESH)
    pl.semaphore_wait(barrier, ROWS + QUAD - 1)


class Gathering:
    AHEAD = 3

    def __init__(self, blocks, wholes, apart, joined, gain_pair, rel_pair, own_blocks, sems):
        self.blocks, self.wholes, self.own_blocks = blocks, wholes, own_blocks
        self.dp, self.quarter, self.row, self.col = place()
        self.partner = (self.dp, self.row, 1 - self.col)
        (
            self.z_send,
            self.z_recv,
            self.q_send,
            self.q_recv,
            self.c_send,
            self.c_recv,
            local_sem,
            s_send,
            s_recv,
        ) = sems
        self.started = []
        count, swaps = len(blocks), len(apart)
        row, col, quarter = self.row, self.col, self.quarter
        greet_all(self.dp, quarter, row, col)
        self.own = {}
        self.from_partner = {}

        def keep(src, dst, slot):
            local = pltpu.make_async_copy(src, dst, local_sem.at[slot])
            local.start()
            self.own[slot] = local

        def half(ref):
            return ref.at[col]

        def rel_at(r):
            return rel_pair[1].at[
                pl.ds(pl.multiple_of(r * 8, 8), 8), pl.ds(pl.multiple_of(col * 128, 128), 128)
            ]

        self.rel_at = rel_at
        self.swap = []
        for j in range(swaps):
            self.swap.append(
                self.remote(
                    apart[j].at[1 - col], half(joined[j]), s_send.at[j], s_recv.at[j], self.partner
                )
            )
            keep(apart[j].at[col], half(joined[j]), count + j)
        self.swap.append(
            self.remote(
                gain_pair[0], half(gain_pair[1]), s_send.at[swaps], s_recv.at[swaps], self.partner
            )
        )
        keep(gain_pair[0], half(gain_pair[1]), count + swaps)
        keep(rel_pair[0], rel_at(row), count + swaps + 1)
        self.rel_sems = (s_send, s_recv, swaps + 1)
        self.rel_copies = [
            self.remote(
                rel_pair[0],
                rel_at(row),
                s_send.at[swaps + 1 + s],
                s_recv.at[swaps + 1 + s],
                self.partner if s == 0 else (self.dp, (row + s) % ROWS, col),
            )
            for s in range(ROWS)
        ]
        self.z_copies = {}
        self.q_copies = {}
        self.local_sem = local_sem
        for i in range(self.AHEAD):
            self.offer(i)
        for i in range(count):
            keep(blocks[i], own_blocks[i], i)

    def offer(self, i):
        row, col = self.row, self.col
        whole_block = self.wholes[i].at[col, pl.ds(pl.multiple_of(row * BLOCK, BLOCK), BLOCK)]
        for s in range(1, ROWS):
            self.z_copies[(i, s)] = self.remote(
                self.blocks[i].at[pl.ds(pl.multiple_of(self.quarter * PIECE, PIECE), PIECE), :],
                self.part(i, row, self.quarter),
                self.z_send.at[i, s - 1],
                self.z_recv.at[i, s - 1],
                (self.dp, (row + s) % ROWS, col),
            )
        self.from_partner[(i, 0, 0)] = self.remote(
            self.blocks[i],
            whole_block,
            self.c_send.at[i, 0, 0],
            self.c_recv.at[i, 0, 0],
            self.partner,
        )

    def remote(self, src, dst, send_sem, recv_sem, device):
        copy = pltpu.make_async_remote_copy(
            src_ref=src,
            dst_ref=dst,
            send_sem=send_sem,
            recv_sem=recv_sem,
            device_id=device,
            device_id_type=MESH,
        )
        copy.start()
        self.started.append(copy)
        return copy

    def part(self, i, r, q):
        at = pl.multiple_of(r * BLOCK + q * PIECE, PIECE)
        return self.wholes[i].at[self.col, pl.ds(at, PIECE)]

    def rel_onward(self):
        s_send, s_recv, base = self.rel_sems
        for s in range(1, ROWS):
            self.rel_copies[s].wait_recv()
            ref = self.rel_at((self.row - s + ROWS) % ROWS)
            slot = base + ROWS - 1 + s
            self.rel_copies.append(
                self.remote(ref, ref, s_send.at[slot], s_recv.at[slot], self.partner)
            )

    def rel_arrived(self, slot):
        self.own[slot].wait()
        self.rel_copies[0].wait_recv()
        for copy in self.rel_copies[ROWS:]:
            copy.wait_recv()

    def hand_over(self, i, s, k, r):
        ref = self.part(i, r, self.quarter ^ k)
        self.from_partner[(i, s, k)] = self.remote(
            ref, ref, self.c_send.at[i, s, k], self.c_recv.at[i, s, k], self.partner
        )

    def to_mate(self, i, s, k, slot, ref):
        self.q_copies[(i, s, slot)] = self.remote(
            ref,
            ref,
            self.q_send.at[i, s - 1, slot - 1],
            self.q_recv.at[i, s - 1, slot - 1],
            (quad_mate(self.dp, self.quarter, k), self.row, self.col),
        )

    def spread(self, i):
        for s in range(1, ROWS):
            self.z_copies[(i, s)].wait_recv()
            r = (self.row - s + ROWS) % ROWS
            ref = self.part(i, r, self.quarter)
            for k in (1, 2):
                self.to_mate(i, s, k, k, ref)
            self.hand_over(i, s, 0, r)
        if i + self.AHEAD < len(self.blocks):
            self.offer(i + self.AHEAD)
        self.own[i].wait()
        self.own[i] = pltpu.make_async_copy(
            self.own_blocks[i],
            self.wholes[i].at[self.col, pl.ds(pl.multiple_of(self.row * BLOCK, BLOCK), BLOCK)],
            self.local_sem.at[i],
        )
        self.own[i].start()

    def share(self, i):
        for s in range(1, ROWS):
            r = (self.row - s + ROWS) % ROWS
            onward = 1 + (i + s) % 2
            for k in (onward, 3 - onward):
                self.q_copies[(i, s, k)].wait_recv()
                if k == onward:
                    self.to_mate(i, s, 3 - k, 3, self.part(i, r, self.quarter ^ k))
                self.hand_over(i, s, k, r)

    def close(self, i):
        for s in range(1, ROWS):
            self.q_copies[(i, s, 3)].wait_recv()
            self.hand_over(i, s, 3, (self.row - s + ROWS) % ROWS)

    def arrived(self, i):
        self.own[i].wait()
        for s in range(ROWS):
            for k in range(QUAD if s else 1):
                self.from_partner[(i, s, k)].wait_recv()

    def finish(self):
        for copy in self.started:
            copy.wait_send()


def forward_body(count, swaps, *refs):
    blocks = refs[:count]
    apart = refs[count : count + swaps]
    gain_in, rel_in, onehot_ref, piece_ref = refs[count + swaps : count + swaps + 4]
    refs = refs[count + swaps + 4 :]
    wholes = refs[:count]
    outs = refs[count : count + 9 + swaps + 1]
    refs = refs[count + 9 + swaps + 1 :]
    h2, rel_all, gains, rows_in, enc, cot, w_qkv, w_out, w_cq, w_ckv, w_co = refs[:11]
    qkv, a1, h1, q2, kv2, a2, t8, lse1, lse2, table, load_sem, save_sem = refs[11:23]
    own_blocks = refs[23 : 23 + count]
    joined = (rows_in, enc, cot)
    comm = Gathering(
        blocks,
        wholes,
        apart,
        joined,
        (gain_in, gains),
        (rel_in, rel_all),
        own_blocks,
        refs[23 + count :],
    )
    saving = []

    class Loads(list):
        def wait(self):
            for copy in self:
                copy.wait()

    def load(src, dst, slot):
        wide = src.shape[2]
        copies = Loads()
        for c in range(2):
            copies.append(
                pltpu.make_async_copy(
                    src.at[c], dst.at[:, c * wide : (c + 1) * wide], load_sem.at[slot, c]
                )
            )
            copies[-1].start()
        return copies

    def save(slot, src):
        copy = pltpu.make_async_copy(src, outs[slot], save_sem.at[slot])
        copy.start()
        saving.append(copy)

    def weight(i, dst):
        comm.arrived(i)
        return load(wholes[i], dst, 3 + i)

    def swapped(j, slot, ref):
        comm.swap[j].wait_recv()
        comm.own[count + j].wait()
        save(slot, ref)

    comm.rel_onward()
    comm.spread(0)
    comm.spread(1)
    swapped(0, 9, rows_in)
    swapped(swaps, 9 + swaps, gains)
    g_self = jnp.concatenate([gains[0, 0:1, :], gains[1, 0:1, :]], axis=1)
    g_cross = jnp.concatenate([gains[0, 1:2, :], gains[1, 1:2, :]], axis=1)
    comm.share(0)
    comm.spread(2)
    step = 256
    blocks_of = [slice(step * b, step * (b + 1)) for b in range(L // step)]
    comm.rel_arrived(count + swaps + 1)
    rel16 = jnp.concatenate([rel_all[:, :6], rel_all[:, 128:134]], axis=1).astype(bf16)
    bias = dot(rel16, onehot_ref[...], TN)
    for n in range(8):
        moved = pltpu.roll(bias, n, 1) if n else bias
        for h in range(12):
            t8[h, n : n + 1, :] = moved[h : h + 1]
    save(0, t8)
    comm.share(1)
    comm.close(0)
    loading = weight(0, w_qkv)
    comm.share(2)
    loading.wait()
    for n, at in enumerate(blocks_of):
        xb = jnp.concatenate([rows_in[0, at, :], rows_in[1, at, :]], axis=1).astype(f32)
        n1 = (xb * rms_of(xb) * g_self).astype(bf16)
        qkv[at, :] = dot(n1, w_qkv[...], NN).astype(bf16)
        if n == 0:
            comm.close(1)
        if n == 1:
            comm.spread(3)
        if n == 2:
            comm.close(2)
        if n == 3:
            comm.share(3)
    save(1, qkv)

    def lane(block):
        return pl.ds(pl.multiple_of(block * 128, 128), 128)

    def self_heads(hp, carry):
        base = (hp // 3) * 9 + (hp % 3) * 3
        self_forward_body(
            piece_ref,
            qkv.at[:, lane(base)],
            qkv.at[:, lane(base + 1)],
            qkv.at[:, lane(base + 2)],
            t8.at[pl.ds(2 * hp, 2)],
            a1.at[:, lane(hp)],
            lse1.at[pl.ds(hp, 1)],
            [table.at[0], table.at[1]],
        )
        return carry

    lax.fori_loop(0, 2, self_heads, 0)
    comm.spread(4)
    comm.close(3)
    loadings = [weight(1, w_out), weight(2, w_cq)]
    swapped(1, 10, enc)
    swapped(2, 11, cot)
    lax.fori_loop(2, 4, self_heads, 0)
    comm.share(4)
    loadings.append(weight(3, w_ckv))
    lax.fori_loop(4, 6, self_heads, 0)
    save(2, a1)
    save(3, lse1)
    comm.close(4)
    comm.spread(5)
    for copy in loadings:
        copy.wait()
    loading = weight(4, w_co)
    kv2[...] = dot(jnp.concatenate([enc[0], enc[1]], axis=1), w_ckv[...], NN).astype(bf16)
    save(6, kv2)
    for n, at in enumerate(blocks_of):
        xb = jnp.concatenate([rows_in[0, at, :], rows_in[1, at, :]], axis=1).astype(f32)
        h1b = xb + dot(a1[at, :], w_out[...], NT)
        h1[at, :] = h1b
        n2 = (h1b * rms_of(h1b) * g_cross).astype(bf16)
        q2[at, :] = dot(n2, w_cq[...], NN).astype(bf16)
    save(4, h1)
    save(5, q2)

    def cross_heads(hp, carry):
        base = (hp // 3) * 6 + hp % 3
        cross_forward_body(
            q2.at[:, lane(hp)],
            kv2.at[:, lane(base)],
            kv2.at[:, lane(base + 3)],
            a2.at[:, lane(hp)],
            lse2.at[pl.ds(hp, 1)],
        )
        return carry

    lax.fori_loop(0, 2, cross_heads, 0)
    comm.spread(6)
    comm.share(5)
    lax.fori_loop(2, 6, cross_heads, 0)
    save(7, a2)
    save(8, lse2)
    comm.close(5)
    loading.wait()
    for at in blocks_of:
        h2[at, :] = h1[at, :] + dot(a2[at, :], w_co[...], NT)
    comm.share(6)
    comm.close(6)
    comm.arrived(5)
    comm.arrived(6)
    for copy in saving:
        copy.wait()
    comm.finish()


def forward(blocks, apart, gains, rel, onehot, piece, number):
    count = len(blocks)
    swaps = len(apart)
    shape = jax.ShapeDtypeStruct
    saved = [
        shape((12, 8, SPAN), f32),
        shape((L, 3 * D), bf16),
        shape((L, D), bf16),
        shape((6, 2, L), f32),
        shape((L, D), f32),
        shape((L, D), bf16),
        shape((LE, 2 * D), bf16),
        shape((L, D), bf16),
        shape((6, 2, L), f32),
    ]
    saved += [shape(x.shape, x.dtype) for x in apart] + [shape((2, 8, HALF), f32)]
    wholes = [shape((2, D, b.shape[1]), b.dtype) for b in blocks]
    dma = pltpu.SemaphoreType.DMA
    any_spec = pl.BlockSpec(memory_space=pl.ANY)
    vmem = pl.BlockSpec(memory_space=pltpu.VMEM)
    scratch = [
        pltpu.VMEM((BUCKETS, 256), f32),
        pltpu.VMEM((2, 8, HALF), f32),
        pltpu.VMEM((2, L, HALF), bf16),
        pltpu.VMEM((2, LE, HALF), bf16),
        pltpu.VMEM((2, L, HALF), bf16),
        pltpu.VMEM((D, 3 * D), bf16),
        pltpu.VMEM((D, D), bf16),
        pltpu.VMEM((D, D), bf16),
        pltpu.VMEM((D, 2 * D), bf16),
        pltpu.VMEM((D, D), bf16),
        pltpu.VMEM((L, 3 * D), bf16),
        pltpu.VMEM((L, D), bf16),
        pltpu.VMEM((L, D), f32),
        pltpu.VMEM((L, D), bf16),
        pltpu.VMEM((LE, 2 * D), bf16),
        pltpu.VMEM((L, D), bf16),
        pltpu.VMEM((12, 8, SPAN), f32),
        pltpu.VMEM((6, 2, L), f32),
        pltpu.VMEM((6, 2, L), f32),
        pltpu.VMEM((2, 128, SPAN), f32),
        dma((8, 2)),
        dma((9 + swaps + 1,)),
    ]
    scratch += [pltpu.VMEM(b.shape, b.dtype) for b in blocks]
    scratch += [
        dma((count, ROWS - 1)),
        dma((count, ROWS - 1)),
        dma((count, ROWS - 1, QUAD - 1)),
        dma((count, ROWS - 1, QUAD - 1)),
        dma((count, ROWS, QUAD)),
        dma((count, ROWS, QUAD)),
        dma((count + swaps + 2,)),
        dma((swaps + 8,)),
        dma((swaps + 8,)),
    ]
    out = pl.pallas_call(
        lambda *refs: forward_body(count, swaps, *refs),
        out_shape=wholes + saved + [shape((L, D), f32)],
        in_specs=[any_spec] * (count + swaps + 2)
        + [vmem, pl.BlockSpec(memory_space=pltpu.SMEM)],
        out_specs=[any_spec] * (len(wholes) + len(saved)) + [vmem],
        scratch_shapes=scratch,
        compiler_params=pltpu.CompilerParams(
            collective_id=number, has_side_effects=True, vmem_limit_bytes=VMEM_LIMIT
        ),
        name="forward",
    )(*blocks, *apart, gains, rel, onehot, piece)
    return (out[:count], out[count + 9 : -1], out[count : count + 9] + out[-1:])


def rms_of(v):
    return lax.rsqrt(jnp.sum(v * v, axis=-1, keepdims=True) * (1.0 / D) + EPSILON)


def norm_back_rows(v, r, gain, dn):
    inner = jnp.sum(dn * gain * v, axis=-1, keepdims=True)
    dv = dn * gain * r - v * (r * r * r) * (inner * (1.0 / D))
    return (dv, jnp.sum(dn * v * r, axis=0, keepdims=True))


def ffn_body(
    h2_ref,
    cot_ref,
    gain_ref,
    wgu_ref,
    wd_ref,
    out_ref,
    dh2_ref,
    ggu_ref,
    gd_ref,
    dgain_ref,
    n3t,
    mid_all,
    e3t,
    dgu_all,
):
    step = pl.program_id(0)
    rows = h2_ref.shape[0]
    here = pl.ds(pl.multiple_of(step * rows, rows), rows)
    g_ffn = jnp.concatenate([gain_ref[0, 2:3, :], gain_ref[1, 2:3, :]], axis=1)
    g_final = jnp.concatenate([gain_ref[0, 3:4, :], gain_ref[1, 3:4, :]], axis=1)
    h2 = h2_ref[...]
    r3 = rms_of(h2)
    n3 = (h2 * r3 * g_ffn).astype(bf16)
    n3t[:, here] = transposed(n3)
    kept = []
    for c in range(4):
        at = (c % 2) * 512
        gate = dot(n3, wgu_ref[c // 2, :, at : at + 512], NN)
        up = dot(n3, wgu_ref[c // 2, :, at + 1024 : at + 1536], NN)
        act, slope = gelu_parts(gate)
        mid = (act * up).astype(bf16)
        mid_all[here, 512 * c : 512 * (c + 1)] = mid
        kept.append((act, up * slope))
    h3 = h2 + dot(mid_all[here, :1024], wd_ref[0], NT) + dot(mid_all[here, 1024:], wd_ref[1], NT)
    r4 = rms_of(h3)
    normed = (h3 * r4 * g_final).astype(bf16)
    out_ref[0] = normed[:, :HALF]
    out_ref[1] = normed[:, HALF:]
    dh3, dg_final = norm_back_rows(h3, r4, g_final, jnp.concatenate([cot_ref[0], cot_ref[1]], axis=1).astype(f32))
    e3 = dh3.astype(bf16)
    e3t[:, here] = transposed(e3)
    for c in range(4):
        at = (c // 2) * 2048 + (c % 2) * 512
        act, slope = kept[c]
        low = 512 * (c % 2)
        dmid = dot(e3, wd_ref[c // 2, :, low : low + 512], NN).astype(bf16).astype(f32)
        dgu_all[here, at : at + 512] = (dmid * slope).astype(bf16)
        dgu_all[here, at + 1024 : at + 1536] = (dmid * act).astype(bf16)
    dn3 = dot(dgu_all[here, :2048], wgu_ref[0], NT) + dot(dgu_all[here, 2048:], wgu_ref[1], NT)
    back, dg_ffn = norm_back_rows(h2, r3, g_ffn, dn3)
    dh2_ref[...] = dh3 + back

    @pl.when(step == 0)
    def _():
        dgain_ref[...] = jnp.zeros_like(dgain_ref)

    dgain_ref[2:3, :] += dg_ffn
    dgain_ref[3:4, :] += dg_final

    @pl.when(step == pl.num_programs(0) - 1)
    def _():
        for c in range(8):
            span = slice(512 * c, 512 * (c + 1))
            low = slice(512 * (c % 4), 512 * (c % 4 + 1))
            ggu_ref[c // 4, :, low] = dot(n3t[...], dgu_all[:, span], NN).astype(bf16)
        for c in range(4):
            span = slice(512 * c, 512 * (c + 1))
            low = slice(512 * (c % 2), 512 * (c % 2 + 1))
            gd_ref[c // 2, :, low] = dot(e3t[...], mid_all[:, span], NN).astype(bf16)


def feed_forward(h2, cot, gains, wgu, wd):
    rows = 256
    def whole(*shape):
        return pl.BlockSpec(shape, lambda i: (0,) * len(shape), pipeline_mode=pl.Buffered(1))

    block = pl.BlockSpec((rows, D), lambda i: (i, 0))
    return pl.pallas_call(
        ffn_body,
        grid=(L // rows,),
        in_specs=[
            block,
            pl.BlockSpec((2, rows, HALF), lambda i: (0, i, 0)),
            whole(2, 8, HALF),
            whole(2, D, 2048),
            whole(2, D, 1024),
        ],
        out_specs=[
            pl.BlockSpec((2, rows, HALF), lambda i: (0, i, 0)),
            block,
            whole(2, D, 2048),
            whole(2, D, 1024),
            whole(8, D),
        ],
        out_shape=[
            jax.ShapeDtypeStruct((2, L, HALF), bf16),
            jax.ShapeDtypeStruct((L, D), f32),
            jax.ShapeDtypeStruct((2, D, 2048), bf16),
            jax.ShapeDtypeStruct((2, D, 1024), bf16),
            jax.ShapeDtypeStruct((8, D), f32),
        ],
        scratch_shapes=[
            pltpu.VMEM((D, L), bf16),
            pltpu.VMEM((L, 2048), bf16),
            pltpu.VMEM((D, L), bf16),
            pltpu.VMEM((L, 4096), bf16),
        ],
        compiler_params=pltpu.CompilerParams(vmem_limit_bytes=VMEM_LIMIT),
        name="feed_forward",
    )(h2, cot, gains, wgu, wd)


class Summing:
    def __init__(self, widths, pair, first, second, third, final, outs, sems):
        self.widths = widths
        self.pair, self.first, self.second, self.third = pair, first, second, third
        self.final, self.outs = final, outs
        self.sends, self.recvs, self.local_sem = sems
        self.dp, self.quarter, self.row, self.col = place()
        self.partner = (self.dp, self.row, 1 - self.col)
        self.begun = []
        self.pending = {}
        self.kept = []
        greet_all(self.dp, self.quarter, self.row, self.col)

    def remote(self, src, dst, send_sem, recv_sem, device):
        copy = pltpu.make_async_remote_copy(
            src_ref=src,
            dst_ref=dst,
            send_sem=send_sem,
            recv_sem=recv_sem,
            device_id=device,
            device_id_type=MESH,
        )
        copy.start()
        self.begun.append(copy)
        return copy

    def send(self, i, slot, src, dst, device):
        self.pending[(i, slot)] = self.remote(
            src, dst, self.sends.at[i, slot], self.recvs.at[i, slot], device
        )

    def mate(self, k):
        return (quad_mate(self.dp, self.quarter, k), self.row, self.col)

    def offer(self, i, src):
        self.send(i, 0, src, self.pair[i], self.partner)

    def stage1(self, i, own):
        self.pending[(i, 0)].wait_recv()
        pair = self.pair[i]
        for r in range(ROWS):
            pair[r] = pair[r] + own(r)
            if r % 2 == 1:
                k = 1 if r == 1 else 2
                for j, q in enumerate((self.quarter ^ k, self.quarter ^ 3)):
                    self.send(
                        i,
                        r + j,
                        pair.at[pl.ds(r - 1, 2), q],
                        self.first[i].at[pl.ds(r - 1, 2), j],
                        self.mate(k),
                    )

    def stage2(self, i):
        first, pair = self.first[i], self.pair[i]
        for h in range(2):
            k = 1 if h == 0 else 2
            self.pending[(i, 1 + 2 * h)].wait_recv()
            self.pending[(i, 2 + 2 * h)].wait_recv()
            for r in (2 * h, 2 * h + 1):
                first[r, 1] = first[r, 1] + pair[r, self.quarter ^ 3 ^ k]
            self.send(
                i,
                5 + h,
                first.at[pl.ds(2 * h, 2), 1],
                self.second[i].at[pl.ds(2 * h, 2)],
                self.mate(3 ^ k),
            )
            for r in (2 * h, 2 * h + 1):
                first[r, 0] = first[r, 0] + pair[r, self.quarter]

    def stage3(self, i):
        second = self.second[i]
        for h in range(2):
            self.pending[(i, 5 + h)].wait_recv()
            for r in (2 * h, 2 * h + 1):
                second[r] = second[r] + self.first[i][r, 0]
        for s in range(1, ROWS):
            to = (self.row + s) % ROWS
            self.send(i, 6 + s, second.at[to], self.third[i].at[s - 1], (self.dp, to, self.col))

    def stage4(self, i):
        for s in range(1, ROWS):
            self.pending[(i, 6 + s)].wait_recv()
        total = self.second[i][self.row].astype(f32)
        for s in range(1, ROWS):
            total = total + self.third[i][s - 1].astype(f32)
        self.final[i][...] = total.astype(bf16)
        there = self.outs[i].at[self.quarter]
        for k in (1, 2):
            self.send(i, 9 + k, self.final[i], there, self.mate(k))
        copy = pltpu.make_async_copy(self.final[i], there, self.local_sem.at[i])
        copy.start()
        self.kept.append(copy)

    def stage5(self, i):
        onward = 1 + i % 2
        for k in (onward, 3 - onward):
            self.pending[(i, 9 + k)].wait_recv()
            if k == onward:
                ref = self.outs[i].at[self.quarter ^ k]
                self.send(i, 12, ref, ref, self.mate(3 - k))

    def finish(self):
        for i in range(len(self.widths)):
            self.pending[(i, 12)].wait_recv()
        for copy in self.kept:
            copy.wait()
        for copy in self.begun:
            copy.wait_send()


CHUNKS = (1024, 1024, 1024, HALF, HALF, 2 * HALF, HALF, HALF, HALF, HALF)
(F0, F1, F2, CO, CQ, CKV, SO, QA, QB, QC) = range(10)
SMALL = (16, 896)


def backward_body(*refs):
    (
        dh2_in,
        g_gu,
        g_down,
        t8_in,
        qkv_in,
        a1_in,
        lse1_in,
        h1_in,
        q2_in,
        kv2_in,
        a2_in,
        lse2_in,
        x_in,
        enc_in,
        w_qkv_in,
        w_out_in,
        w_cq_in,
        w_ckv_in,
        w_co_in,
        made,
        gains,
        ffn_gains,
        onehot_ref,
        piece_ref,
    ) = refs[:24]
    count = len(CHUNKS)
    output, hidden_grad, enc_grad = refs[24:27]
    sums = refs[27 : 27 + count]
    small_out = refs[27 + count]
    refs = refs[28 + count :]
    pair = refs[:count]
    first = refs[count : 2 * count]
    second = refs[2 * count : 3 * count]
    third = refs[3 * count : 4 * count]
    final = refs[4 * count : 5 * count]
    refs = refs[5 * count :]
    gr_co, gr_cq, gr_ckv, gr_out, gr_qkv = refs[:5]
    total, turned, mixed, dmixed, w_big, w_cq, w_out, enc, rows, qkv, t8, lse1, lse2, x = refs[5:19]
    dk_sum, dv_sum, diag, spans_all, eg, small = refs[19:25]
    load_sem, ex_send, ex_recv, ex_local, small_send, small_recv = refs[25:31]
    comm = Summing(CHUNKS, pair, first, second, third, final, sums, refs[31:34])
    col, row, partner = comm.col, comm.row, comm.partner

    def load(slot, *pairs):
        copies = []
        for n, (src, dst) in enumerate(pairs):
            copies.append(pltpu.make_async_copy(src, dst, load_sem.at[slot, n]))
            copies[-1].start()
        return copies

    def wait(copies):
        for copy in copies:
            copy.wait()

    def halves(src, dst, offset=0):
        wide = src.shape[2]
        return [
            (src.at[c], dst.at[:, offset + c * wide : offset + (c + 1) * wide]) for c in range(2)
        ]

    def own_ffn(i):
        src = (g_gu, g_gu, g_down)[i]
        lanes_of = pl.ds(1024 if i == 1 else 0, 1024)
        slot = i % 2
        return load(
            12 + i,
            *[
                (
                    src.at[col, r, :, :, lanes_of],
                    gr_qkv.at[slot * 4 + r, :, :, pl.ds(0, 1024)],
                )
                for r in range(ROWS)
            ],
        )

    bouncing = load(0, (made.at[col], dmixed.at[:, :HALF]))
    ex_out = comm.remote(
        made.at[1 - col], output.at[col], ex_send.at[0], ex_recv.at[0], partner
    )
    comm.offer(F0, g_gu.at[1 - col, :, :, :, pl.ds(0, 1024)])
    comm.offer(F1, g_gu.at[1 - col, :, :, :, pl.ds(1024, 1024)])
    comm.offer(F2, g_down.at[1 - col])
    l_total = load(1, (dh2_in, total))
    l_co = load(2, *halves(w_co_in, w_big, 2 * D))
    l_a2 = load(3, (a2_in, mixed))
    l_own = [own_ffn(0), own_ffn(1)]
    l_q2 = load(4, (q2_in, qkv.at[:, :D]), (kv2_in, qkv.at[:LE, D:]), (lse2_in, lse2))
    l_h1 = load(
        5, *[(h1_in.at[pl.ds(512 * n, 512)], rows.at[:, D * n : D * (n + 1)]) for n in range(2)]
    )
    l_ckv = load(6, *halves(w_ckv_in, w_big))
    l_cq = load(7, *halves(w_cq_in, w_cq))
    l_enc = load(8, *halves(enc_in, enc))
    l_out = load(9, *halves(w_out_in, w_out))
    l_x = load(10, *halves(x_in, x))
    l_t8 = load(11, (t8_in, t8), (lse1_in, lse1))

    step = 256
    blocks_of = [slice(step * b, step * (b + 1)) for b in range(L // step)]
    g_self = jnp.concatenate([gains[0, 0:1, :], gains[1, 0:1, :]], axis=1)
    g_cross = jnp.concatenate([gains[0, 1:2, :], gains[1, 1:2, :]], axis=1)

    def lane(block):
        if isinstance(block, int):
            return pl.ds(block * 128, 128)
        return pl.ds(pl.multiple_of(block * 128, 128), 128)

    def put(dst, value):
        dst[...] = value.astype(bf16).reshape(dst.shape)

    def own_of(ref):
        return lambda r: ref[col, r]

    def own_loaded(i):
        slot = i % 2
        return lambda r: gr_qkv[slot * 4 + r, :, :, pl.ds(0, 1024)]

    wait(bouncing)
    keep_out = pltpu.make_async_copy(dmixed.at[:, :HALF], output.at[col], ex_local.at[0])
    keep_out.start()
    wait(l_total)
    for at in blocks_of:
        turned[:, at] = transposed(total[at, :])
    wait(l_co)
    keep_out.wait()
    for at in blocks_of:
        dmixed[at, :] = dot(total[at, :].astype(bf16), w_big[:, 2 * D :], NN).astype(bf16)
    wait(l_a2)
    for c in range(2):
        put(gr_co.at[c], dot(turned[...], mixed[:, HALF * c : HALF * (c + 1)], NN))
    comm.offer(CO, gr_co.at[1 - col])
    wait(l_own[0])
    comm.stage1(F0, own_loaded(0))
    wait(l_q2)

    def cross_heads(hp, carry):
        base = 6 + (hp // 3) * 6 + hp % 3
        queries = qkv.at[:, lane(hp)]
        keys = qkv.at[pl.ds(0, LE), lane(base)]
        values = qkv.at[pl.ds(0, LE), lane(base + 3)]
        cross_backward_body(
            queries,
            keys,
            values,
            mixed.at[:, lane(hp)],
            dmixed.at[:, lane(hp)],
            lse2.at[pl.ds(hp, 1)],
            queries,
            keys,
            values,
        )
        return carry

    lax.fori_loop(0, 2, cross_heads, 0)
    wait(l_own[1])
    comm.stage1(F1, own_loaded(1))
    l_own.append(own_ffn(2))
    lax.fori_loop(2, 4, cross_heads, 0)
    comm.stage2(F0)
    wait(l_own[2])
    comm.stage1(F2, own_loaded(2))
    comm.stage1(CO, own_of(gr_co))
    lax.fori_loop(4, 6, cross_heads, 0)
    l_a1 = load(3, (a1_in, mixed))
    comm.stage2(F1)
    wait(l_h1)

    def h1_rows(b):
        return rows[256 * (b % 2) : 256 * (b % 2 + 1), D * (b // 2) : D * (b // 2 + 1)]

    for b, at in enumerate(blocks_of):
        h1b = h1_rows(b)
        turned[:, at] = transposed((h1b * rms_of(h1b) * g_cross).astype(bf16))
    for c in range(2):
        put(gr_cq.at[c], dot(turned[...], qkv[:, HALF * c : HALF * (c + 1)], NN))
    comm.offer(CQ, gr_cq.at[1 - col])
    wait(l_enc)
    enct = transposed(enc[...])
    for c in range(2):
        put(gr_ckv.at[c], dot(enct, qkv[:LE, D + D * c : D + D * (c + 1)], NN))
    comm.offer(CKV, gr_ckv.at[1 - col])
    comm.stage2(F2)
    comm.stage3(F0)
    wait(l_ckv)
    back = dot(qkv[:LE, D:], w_big[:, : 2 * D], NT)
    eg[0] = back[:, :HALF]
    eg[1] = back[:, HALF:]
    ex_eg = comm.remote(eg.at[1 - col], enc_grad.at[col], ex_send.at[1], ex_recv.at[1], partner)
    keep_eg = pltpu.make_async_copy(eg.at[col], enc_grad.at[col], ex_local.at[1])
    keep_eg.start()
    l_qkv = load(2, *halves(w_qkv_in, w_big))
    wait(l_cq)
    wait(l_out)
    comm.stage2(CO)
    dg_cross = jnp.zeros((1, D), f32)
    for b, at in enumerate(blocks_of):
        h1b = h1_rows(b)
        dn2 = dot(qkv[at, :D], w_cq[...], NT)
        dv, dg = norm_back_rows(h1b, rms_of(h1b), g_cross, dn2)
        dg_cross = dg_cross + dg
        dh1 = total[at, :] + dv
        total[at, :] = dh1
        e1 = dh1.astype(bf16)
        turned[:, at] = transposed(e1)
        dmixed[at, :] = dot(e1, w_out[...], NN).astype(bf16)
        if b == 1:
            comm.stage3(F1)
            comm.stage1(CQ, own_of(gr_cq))
    l_q1 = load(4, (qkv_in, qkv))
    comm.stage1(CKV, own_of(gr_ckv))
    wait(l_a1)
    for c in range(2):
        put(gr_out.at[c], dot(turned[...], mixed[:, HALF * c : HALF * (c + 1)], NN))
    comm.offer(SO, gr_out.at[1 - col])
    comm.stage3(F2)
    comm.stage3(CO)
    wait(l_x)
    for at in blocks_of:
        xb = x[at, :].astype(f32)
        turned[:, at] = transposed((xb * rms_of(xb) * g_self).astype(bf16))
    wait(l_t8)
    wait(l_q1)
    table = [rows.at[pl.ds(128 * h, 128)] for h in range(2)]
    spans = [rows.at[pl.ds(256 + 128 * h, 128)] for h in range(2)]
    spans_all[...] = jnp.zeros_like(spans_all)

    def self_heads(hp):
        base = 9 * (hp // 3) + 3 * (hp % 3)
        queries, keys, values = [qkv.at[:, lane(base + n)] for n in range(3)]
        self_backward_body(
            piece_ref,
            queries,
            keys,
            values,
            t8.at[pl.ds(2 * hp, 2)],
            mixed.at[:, lane(hp)],
            dmixed.at[:, lane(hp)],
            lse1.at[pl.ds(hp, 1)],
            queries,
            keys,
            values,
            diag,
            table,
            spans,
            dk_sum,
            dv_sum,
        )
        for h in range(2):
            lined = diag[h, 0:1, :]
            for n in range(1, 8):
                lined = lined + pltpu.roll(diag[h, n : n + 1, :], SPAN - n, 1)
            spans_all[pl.ds(2 * hp + h, 1), :] = lined

    def qkv_grad(j, c):
        return gr_qkv.at[pl.ds(4 * c, 4), :, :, pl.ds(HALF * j, HALF)]

    def grads_of(j):
        for c in range(2):
            at = 3 * HALF * c + HALF * j
            put(qkv_grad(j, c), dot(turned[...], qkv[:, at : at + HALF], NN))
        comm.offer(QA + j, qkv_grad(j, 1 - col))

    def own_qkv(j):
        return lambda r: gr_qkv[4 * col + r, :, :, pl.ds(HALF * j, HALF)]

    self_heads(0)
    comm.stage1(SO, own_of(gr_out))
    comm.stage2(CQ)
    comm.stage4(F0)
    self_heads(3)
    comm.stage2(CKV)
    comm.stage4(F1)
    grads_of(0)
    self_heads(1)
    comm.stage1(QA, own_qkv(0))
    comm.stage2(SO)
    comm.stage3(CQ)
    comm.stage3(CKV)
    comm.stage4(F2)
    comm.stage4(CO)
    comm.stage5(F0)
    self_heads(4)
    comm.stage2(QA)
    comm.stage3(SO)
    comm.stage4(CQ)
    comm.stage5(F1)
    grads_of(1)
    self_heads(2)
    comm.stage1(QB, own_qkv(1))
    comm.stage3(QA)
    comm.stage4(CKV)
    comm.stage5(F2)
    comm.stage5(CO)
    self_heads(5)
    comm.stage2(QB)
    comm.stage4(QA)
    comm.stage4(SO)
    comm.stage5(CQ)
    comm.stage5(CKV)
    grads_of(2)
    comm.stage3(QB)

    wait(l_qkv)
    left = spans_all[...]
    rel = jnp.zeros((16, BUCKETS), f32)
    for _ in range(3):
        high = left.astype(bf16)
        rel = rel + dot(high, onehot_ref[...], NT)
        left = left - high.astype(f32)
    dg_self = jnp.zeros((1, D), f32)
    leaving = []

    def half_of(c):
        return pl.ds(pl.multiple_of(c * HALF, 128), HALF)

    for b, at in enumerate(blocks_of):
        xb = x[at, :].astype(f32)
        dn1 = dot(qkv[at, :], w_big[...], NT)
        dv, dg = norm_back_rows(xb, rms_of(xb), g_self, dn1)
        dg_self = dg_self + dg
        total[at, :] = total[at, :] + dv
        leaving.append(
            comm.remote(
                total.at[at, half_of(1 - col)],
                hidden_grad.at[col, at],
                ex_send.at[2 + b],
                ex_recv.at[2 + b],
                partner,
            )
        )
        kept = pltpu.make_async_copy(
            total.at[at, half_of(col)], hidden_grad.at[col, at], ex_local.at[2 + b]
        )
        kept.start()
        comm.kept.append(kept)
        if b == 0:
            comm.stage1(QC, own_qkv(2))
            comm.stage5(QA)
        if b == 1:
            comm.stage4(QB)
        if b == 2:
            comm.stage2(QC)
            comm.stage5(SO)

    small[0] = jnp.zeros(SMALL, f32)
    small[0, 0:1, :D] = dg_self
    small[0, 1:2, :D] = dg_cross
    small[0, 2:4, :D] = ffn_gains[2:4, :]
    small[0, :, D : D + BUCKETS] = rel
    passing = {}

    def pass_on(slot, src, dst, device):
        passing[slot] = comm.remote(
            small.at[src], small.at[dst], small_send.at[slot], small_recv.at[slot], device
        )

    pass_on(0, 0, 1, partner)
    comm.stage3(QC)
    passing[0].wait_recv()
    small[2] = small[0] + small[1]
    pass_on(1, 2, 3, comm.mate(1))
    comm.stage5(QB)
    passing[1].wait_recv()
    small[4] = small[2] + small[3]
    pass_on(2, 4, 5, comm.mate(2))
    comm.stage4(QC)
    passing[2].wait_recv()
    small[6 + row] = small[4] + small[5]
    for s in range(1, ROWS):
        pass_on(2 + s, 6 + row, 6 + row, (comm.dp, (row + s) % ROWS, col))
    comm.stage5(QC)
    for s in range(1, ROWS):
        passing[2 + s].wait_recv()
    small_out[...] = (small[6] + small[7]) + (small[8] + small[9])
    keep_eg.wait()
    ex_out.wait_recv()
    ex_eg.wait_recv()
    for copy in leaving:
        copy.wait_recv()
    comm.finish()


def backward(args, onehot, piece, number):
    shape = jax.ShapeDtypeStruct
    dma = pltpu.SemaphoreType.DMA
    any_spec = pl.BlockSpec(memory_space=pl.ANY)
    vmem = pl.BlockSpec(memory_space=pltpu.VMEM)
    count = len(CHUNKS)
    quarters = (ROWS, QUAD, PIECE)
    scratch = [pltpu.VMEM(quarters + (w,), bf16) for w in CHUNKS]
    scratch += [pltpu.VMEM((ROWS, 2, PIECE, w), bf16) for w in CHUNKS]
    scratch += [pltpu.VMEM((ROWS, PIECE, w), bf16) for w in CHUNKS]
    scratch += [pltpu.VMEM((ROWS - 1, PIECE, w), bf16) for w in CHUNKS]
    scratch += [pltpu.VMEM((PIECE, w), bf16) for w in CHUNKS]
    scratch += [
        pltpu.VMEM((2,) + quarters + (HALF,), bf16),
        pltpu.VMEM((2,) + quarters + (HALF,), bf16),
        pltpu.VMEM((2,) + quarters + (2 * HALF,), bf16),
        pltpu.VMEM((2,) + quarters + (HALF,), bf16),
        pltpu.VMEM((2 * ROWS, QUAD, PIECE, 3 * HALF), bf16),
        pltpu.VMEM((L, D), f32),
        pltpu.VMEM((D, L), bf16),
        pltpu.VMEM((L, D), bf16),
        pltpu.VMEM((L, D), bf16),
        pltpu.VMEM((D, 3 * D), bf16),
        pltpu.VMEM((D, D), bf16),
        pltpu.VMEM((D, D), bf16),
        pltpu.VMEM((LE, D), bf16),
        pltpu.VMEM((L // 2, 2 * D), f32),
        pltpu.VMEM((L, 3 * D), bf16),
        pltpu.VMEM((12, 8, SPAN), f32),
        pltpu.VMEM((6, 2, L), f32),
        pltpu.VMEM((6, 2, L), f32),
        pltpu.VMEM((L, D), bf16),
        pltpu.VMEM((L, 128), f32),
        pltpu.VMEM((L, 128), f32),
        pltpu.VMEM((2, 8, SPAN), f32),
        pltpu.VMEM((16, SPAN), f32),
        pltpu.VMEM((2, LE, HALF), f32),
        pltpu.VMEM((6 + ROWS,) + SMALL, f32),
        dma((15, 4)),
        dma((6,)),
        dma((6,)),
        dma((6,)),
        dma((6,)),
        dma((6,)),
        dma((count, 13)),
        dma((count, 13)),
        dma((count,)),
    ]
    out = pl.pallas_call(
        backward_body,
        out_shape=[
            shape((2, L, HALF), bf16),
            shape((2, L, HALF), f32),
            shape((2, LE, HALF), f32),
        ]
        + [shape((QUAD, PIECE, w), bf16) for w in CHUNKS]
        + [shape(SMALL, f32)],
        in_specs=[any_spec] * 20
        + [vmem] * 3
        + [pl.BlockSpec(memory_space=pltpu.SMEM)],
        out_specs=[any_spec] * (3 + count) + [vmem],
        scratch_shapes=scratch,
        compiler_params=pltpu.CompilerParams(
            collective_id=number, has_side_effects=True, vmem_limit_bytes=VMEM_LIMIT
        ),
        name="backward",
    )(*args, onehot, piece)
    return (out[:3], [o.reshape(BLOCK, o.shape[2]) for o in out[3:-1]], out[-1])


def inverse_rms(v):
    return lax.rsqrt(jnp.mean(v * v, axis=-1, keepdims=True) + EPSILON)


def norm_backward(v, r, gain, dn):
    inner = jnp.sum(dn * gain * v, axis=-1, keepdims=True)
    dv = dn * gain * r - v * (r * r * r) * (inner / D)
    return (dv, jnp.sum(dn * v * r, axis=0))


def gelu_parts(t):
    inner = ROOT_TWO_PI * (t + 0.044715 * t * t * t)
    th = jnp.tanh(inner)
    value = 0.5 * t * (1.0 + th)
    slope = 0.5 * (1.0 + th) + 0.5 * t * (1.0 - th * th) * ROOT_TWO_PI * (
        1.0 + 3.0 * 0.044715 * t * t
    )
    return (value, slope)


def body(
    quads,
    hidden_in,
    encoded,
    cotangent,
    piece_start,
    image_piece_lengths,
    bucket_table,
    self_query,
    self_key,
    self_value,
    self_out,
    rel_weight,
    cross_query,
    cross_key,
    cross_value,
    cross_out,
    ffn_gate,
    ffn_up,
    ffn_down,
    gain_self,
    gain_cross,
    gain_ffn,
    gain_final,
):
    col = lax.axis_index("col")
    row = lax.axis_index("row")
    blocks = (
        jnp.stack(
            [w.reshape(BLOCK, 3, 128) for w in (self_query, self_key, self_value)], axis=2
        ).reshape(BLOCK, 3 * HALF),
        self_out.T,
        cross_query,
        jnp.concatenate([cross_key, cross_value], axis=1),
        cross_out.T,
        jnp.concatenate([ffn_gate, ffn_up], axis=1),
        ffn_down.T,
    )
    gain_block = jnp.stack([gain_self, gain_cross, gain_ffn, gain_final])
    gain_block = jnp.concatenate([gain_block, jnp.zeros_like(gain_block)])
    rel_block = jnp.pad(rel_weight.astype(f32), ((0, 0), (0, 122)))
    turned_table = bucket_table[:SPAN][::-1]
    onehot = (turned_table[None, :] == jnp.arange(BUCKETS, dtype=jnp.int32)[:, None]).astype(bf16)
    starts = lax.dynamic_index_in_dim(piece_start, col, 0, keepdims=False)
    lengths = lax.dynamic_index_in_dim(image_piece_lengths, col, 0, keepdims=False)
    piece = jnp.concatenate([starts, starts + lengths])
    wholes, (x, enc, cot, gains), saved = forward(
        blocks,
        (hidden_in, encoded, cotangent),
        gain_block,
        rel_block,
        onehot,
        piece,
        0,
    )
    t8, qkv, a1, lse1, h1, q2, kv2, a2, lse2, h2 = saved
    made, dh2, gr_gu, gr_down, ffn_gains = feed_forward(h2, cot, gains, wholes[5], wholes[6])
    cut = (2, ROWS, QUAD, PIECE)
    (output, hidden_grad, enc_grad), grads, small = backward(
        (
            dh2,
            gr_gu.reshape(cut + (2048,)),
            gr_down.reshape(cut + (1024,)),
            t8,
            qkv,
            a1,
            lse1,
            h1,
            q2,
            kv2,
            a2,
            lse2,
            x,
            enc,
            *wholes[:5],
            made,
            gains,
            ffn_gains,
        ),
        onehot,
        piece,
        1,
    )
    if quads > 1:
        grads, small = jax.tree.map(
            lambda t: lax.psum(t, "dp") * jnp.asarray(1.0 / QUAD, t.dtype), (grads, small)
        )
    grads = [g.astype(f32) for g in grads]
    gr_gate, gr_up, gr_down, gr_co, gr_cq, gr_ckv, gr_out = grads[:7]
    gr_q, gr_k, gr_v = [
        jnp.concatenate([g[:, 128 * n : 128 * (n + 1)] for g in grads[7:]], axis=1)
        for n in range(3)
    ]
    gain_sums = lax.dynamic_slice_in_dim(small[:4], col * HALF, HALF, 1)
    gr_rel = lax.dynamic_slice(small, (col * 6, D + row * 8), (6, 8)).T
    return (
        output,
        hidden_grad,
        enc_grad,
        gr_q,
        gr_k,
        gr_v,
        gr_out.T,
        gr_rel,
        gr_cq,
        gr_ckv[:, :HALF],
        gr_ckv[:, HALF:],
        gr_co.T,
        gr_gate,
        gr_up,
        gr_down.T,
        gain_sums[0],
        gain_sums[1],
        gain_sums[2],
        gain_sums[3],
    )


def solution(mesh):
    batch = P(("dp", "row"), None, "col")
    inward = P("row", "col")
    outward = P("col", "row")
    gain = P("col")
    weights = (
        (inward,) * 3 + (outward, inward) + (inward,) * 3 + (outward,) + (inward,) * 2 + (outward,)
    )
    placed = (batch,) * 3 + (P(("dp", "row"), None),) * 2 + (P(),) + weights + (gain,) * 4
    return jax.shard_map(
        lambda *args: body(mesh.shape["dp"] // QUAD, *args),
        mesh=mesh,
        in_specs=placed,
        out_specs=(batch,) * 3 + weights + (gain,) * 4,
        check_vma=False,
    )
```

profile of v0, /device:TPU:0, one launch (start us, length us, event | category | flops | bytes accessed | tf_op | source)
XLA Modules:
  0.0 320.1 jit_solution(7575675375092437101)
XLA Ops:
  0.7 0.7 fusion.3
  1.4 0.6 pad_add_fusion.refs_13_.refs_23_
  2.0 0.8 rev.3
  2.7 0.7 fusion.refs_12_.refs_22_
  3.4 1.0 stack_reshape.10
  4.3 1.0 stack_reshape.11
  5.3 1.0 stack_reshape.9
  6.3 0.0 copy-start.3
  6.3 0.0 copy-start.4
  6.3 0.5 pad_maximum_fusion.1
  6.8 0.6 copy.45
  7.4 0.0 copy-start.13
  7.4 0.0 copy-start.14
  7.4 0.0 copy-start.16
  7.4 0.0 copy-start.17
  7.5 0.0 copy-start.18
  7.5 0.0 copy-start.19
  7.5 0.0 copy-start.15
  7.5 1.1 reshape.78.refs_0_
  8.6 0.0 copy-done.3
  8.6 0.0 copy-done.4
  8.6 0.9 pad_maximum_fusion.refs_5_
  9.6 0.0 copy-done.13
  9.6 0.0 copy-done.14
  9.6 0.7 pad_maximum_fusion.2.refs_3_
  10.3 0.0 copy-done.16
  10.3 0.0 copy-done.17
  10.3 0.0 copy-done.18
  10.4 0.0 copy-done.19
  10.4 0.6 concatenate.23.refs_10_
  11.0 0.0 copy-done.15
  11.0 0.6 pad_convert_fusion.refs_11_
  11.6 107.2 %forward.1 = (bf16[2,768,1152]{2,1,0:T(8,128)(2,1)}, bf16[2,768,384]{2,1,0:T(8,128)(2,1)}, bf16[2,768,384]{2,1,0:T(8,128)(2,1)}, bf16[2,768,768]{2,1,0:T(8,128)(...) custom-call(bf16[192,1152]{1,0:T(8,128)(2,1)} %reshape.78.refs_0_, ...), custom_call_target="tpu_custom_call" | custom-call | tf_op jit(solution)/shard_map/forward/pallas_call | solution.py:673
  118.8 59.1 %feed_forward.1 = (bf16[2,1024,384]{2,1,0:T(8,128)(2,1)}, f32[1024,768]{1,0:T(8,128)}, bf16[2,768,2048]{2,1,0:T(8,128)(2,1)}, bf16[2,768,1024]{2,1,0:T(8,128)(2,1)}, f32[8,768]{1,0:T(8,128)}) custom-call(f32[1024,768]{1,0:T(8,128)} %get-tuple-element.59.h2_ref, bf16[2,1024,384]{2,1,0:T(8,128)(2,1)} %get-tuple-element.60.cot_ref, ...), custom_call_target="tpu_custom_call" | custom-call | tf_op jit(solution)/shard_map/feed_forward/pallas_call | solution.py:776
  177.9 125.6 %backward.1 = (bf16[2,1024,384]{2,1,0:T(8,128)(2,1)}, f32[2,1024,384]{2,1,0:T(8,128)}, f32[2,256,384]{2,1,0:T(8,128)}, bf16[4,48,1024]{2,1,0:T(8,128)(2,1)}, bf1...) custom-call(f32[1024,768]{1,0:T(8,128)} %get-tuple-element.64.refs_0, ...), custom_call_target="tpu_custom_call" | custom-call | tf_op jit(solution)/shard_map/backward/pallas_call | solution.py:1360
  303.5 0.0 copy-start.11
  303.5 0.0 copy-start.12
  303.5 0.0 copy-start.9
  303.5 0.0 copy-start.10
  303.6 2.5 convert_bitcast_fusion
  306.0 0.0 copy-done.11
  306.1 0.0 copy-done.12
  306.1 0.9 convert_bitcast_fusion.1
  306.9 0.0 copy-done.9
  306.9 0.0 copy-done.10
  306.9 0.1 bitcast_convert_fusion.5
  307.1 0.0 copy-done.7
  307.1 0.0 copy-done.8
  307.1 0.8 bitcast_convert_fusion.3
  307.9 0.7 pad_maximum_fusion.5
  308.7 0.7 pad_maximum_fusion.4
  309.4 0.7 pad_maximum_fusion.3
  310.1 0.1 bitcast_convert_fusion.2
  310.2 0.9 fusion.5
  311.1 1.0 bitcast_convert_fusion.1
  312.0 0.8 slice.63
  312.8 0.7 dynamic-slice_reduce_fusion
  313.5 0.8 dynamic-slice_bitcast_fusion
  314.2 0.7 copy.46
  314.9 1.1 copy.50
  316.1 1.3 copy-done
  317.4 1.7 copy.51
  319.0 0.0 copy-done.2
  319.1 0.9 copy.52
  (18 shorter events, 0.1 us)
Async XLA Ops:
  6.3 2.4 copy-start.3
  6.3 2.3 copy-start.4
  7.4 2.2 copy-start.13
  7.4 2.2 copy-start.14
  7.4 2.9 copy-start.16
  7.4 2.9 copy-start.17
  7.5 2.9 copy-start.18
  7.5 2.9 copy-start.19
  7.5 3.5 %copy-start.15 = (bf16[8,6]{1,0:T(8,128)(2,1)S(1)}, bf16[8,6]{1,0:T(8,128)(2,1)}, u32[]{:S(2)}) copy-start(bf16[8,6]{1,0:T(8,128)(2,1)} %param.32) | copy-start | bytes 292
  303.5 2.5 copy-start.11
  303.5 2.5 copy-start.12
  303.5 3.4 %copy-start.9 = (bf16[4,48,384]{2,1,0:T(8,128)(2,1)S(1)}, bf16[4,48,384]{2,1,0:T(8,128)(2,1)}, u32[]{:S(2)}) copy-start(bf16[4,48,384]{2,1,0:T(8,128)(2,1)} %get-tuple-element.88) | copy-start | bytes 442372
  303.5 3.4 %copy-start.10 = (bf16[4,48,384]{2,1,0:T(8,128)(2,1)S(1)}, bf16[4,48,384]{2,1,0:T(8,128)(2,1)}, u32[]{:S(2)}) copy-start(bf16[4,48,384]{2,1,0:T(8,128)(2,1)} %get-tuple-element.89) | copy-start | bytes 442372
  306.0 1.0 copy-start.7
  306.0 1.1 copy-start.8
  307.1 3.0 copy-start.6
  308.7 2.4 copy-start.5
  310.1 4.8 %copy-start.1 = (bf16[2,1024,384]{2,1,0:T(8,128)(2,1)S(1)}, bf16[2,1024,384]{2,1,0:T(8,128)(2,1)}, u32[]{:S(2)}) copy-start(bf16[2,1024,384]{2,1,0:T(8,128)(2,1)} %get-tuple-element.181) | copy-start | bytes 4718596
  314.9 2.5 copy-start
  317.4 1.7 copy-start.2
where the time goes:
time: 326 us; the launch traced here: 320 us
  Pallas kernels  292 us (90%)
  local copies, waits for them, and re-layouts  14.9 us (5%)
  other arithmetic  12.2 us (4%)
    pallas_call x1, Pallas kernels, backward(): pl.pallas_call(backward_body, out_shape=[shape((2, L, HALF), bf16), shape...  126 us
    pallas_call x1, Pallas kernels, forward(): pl.pallas_call(lambda *refs: forward_body(count, swaps, *refs), out_shape...  107 us
    pallas_call x1, Pallas kernels, feed_forward(): pl.pallas_call(ffn_body, grid=(L // rows,), in_specs=[block, pl.BlockSpec...  59.1 us

commit v1 on v0

--- a/solution.py
+++ b/solution.py
@@ -262,11 +262,21 @@
     pl.semaphore_wait(barrier, ROWS + QUAD - 1)
 
 
+def rms_of(v):
+    return lax.rsqrt(jnp.sum(v * v, axis=-1, keepdims=True) * (1.0 / D) + EPSILON)
+
+
+def norm_back_rows(v, r, gain, dn):
+    inner = jnp.sum(dn * gain * v, axis=-1, keepdims=True)
+    dv = dn * gain * r - v * (r * r * r) * (inner * (1.0 / D))
+    return (dv, jnp.sum(dn * v * r, axis=0, keepdims=True))
+
+
 class Gathering:
     AHEAD = 3
 
-    def __init__(self, blocks, wholes, apart, joined, gain_pair, rel_pair, own_blocks, sems):
-        self.blocks, self.wholes, self.own_blocks = blocks, wholes, own_blocks
+    def __init__(self, sources, wholes, swaps, rel_pair, sems):
+        self.wholes = wholes
         self.dp, self.quarter, self.row, self.col = place()
         self.partner = (self.dp, self.row, 1 - self.col)
         (
@@ -276,24 +286,30 @@
             self.q_recv,
             self.c_send,
             self.c_recv,
-            local_sem,
+            own_sem,
             s_send,
             s_recv,
+            s_own,
         ) = sems
-        self.started = []
-        count, swaps = len(blocks), len(apart)
-        row, col, quarter = self.row, self.col, self.quarter
-        greet_all(self.dp, quarter, row, col)
-        self.own = {}
-        self.from_partner = {}
-
-        def keep(src, dst, slot):
-            local = pltpu.make_async_copy(src, dst, local_sem.at[slot])
-            local.start()
-            self.own[slot] = local
-
-        def half(ref):
-            return ref.at[col]
+        self.started = {}
+        self.along = {}
+        row, col = self.row, self.col
+        self.own = []
+        for i, parts in enumerate(sources):
+            self.own.append([])
+            for n, (src, to) in enumerate(parts):
+                copy = pltpu.make_async_copy(
+                    src,
+                    wholes[i].at[col, self.own_rows(), pl.ds(to, src.shape[1])],
+                    own_sem.at[i, n],
+                )
+                copy.start()
+                self.own[i].append(copy)
+        self.swap_own = []
+        for j, (src, own, dst) in enumerate(swaps):
+            copy = pltpu.make_async_copy(src if own is None else src.at[own], dst.at[col], s_own.at[j])
+            copy.start()
+            self.swap_own.append(copy)
 
         def rel_at(r):
             return rel_pair[1].at[
@@ -301,60 +317,41 @@
             ]
 
         self.rel_at = rel_at
+        count = len(swaps)
+        self.rel_own = pltpu.make_async_copy(rel_pair[0], rel_at(row), s_own.at[count])
+        self.rel_own.start()
+        greet_all(self.dp, self.quarter, row, col)
         self.swap = []
-        for j in range(swaps):
+        for j, (src, own, dst) in enumerate(swaps):
             self.swap.append(
                 self.remote(
-                    apart[j].at[1 - col], half(joined[j]), s_send.at[j], s_recv.at[j], self.partner
+                    src if own is None else src.at[1 - own],
+                    dst.at[col],
+                    s_send.at[j],
+                    s_recv.at[j],
+                    self.partner,
                 )
             )
-            keep(apart[j].at[col], half(joined[j]), count + j)
-        self.swap.append(
-            self.remote(
-                gain_pair[0], half(gain_pair[1]), s_send.at[swaps], s_recv.at[swaps], self.partner
-            )
-        )
-        keep(gain_pair[0], half(gain_pair[1]), count + swaps)
-        keep(rel_pair[0], rel_at(row), count + swaps + 1)
-        self.rel_sems = (s_send, s_recv, swaps + 1)
+        self.rel_sems = (s_send, s_recv, count)
         self.rel_copies = [
             self.remote(
                 rel_pair[0],
                 rel_at(row),
-                s_send.at[swaps + 1 + s],
-                s_recv.at[swaps + 1 + s],
+                s_send.at[count + s],
+                s_recv.at[count + s],
                 self.partner if s == 0 else (self.dp, (row + s) % ROWS, col),
             )
             for s in range(ROWS)
         ]
-        self.z_copies = {}
         self.q_copies = {}
-        self.local_sem = local_sem
+        self.from_partner = {}
         for i in range(self.AHEAD):
             self.offer(i)
-        for i in range(count):
-            keep(blocks[i], own_blocks[i], i)
-
-    def offer(self, i):
-        row, col = self.row, self.col
-        whole_block = self.wholes[i].at[col, pl.ds(pl.multiple_of(row * BLOCK, BLOCK), BLOCK)]
-        for s in range(1, ROWS):
-            self.z_copies[(i, s)] = self.remote(
-                self.blocks[i].at[pl.ds(pl.multiple_of(self.quarter * PIECE, PIECE), PIECE), :],
-                self.part(i, row, self.quarter),
-                self.z_send.at[i, s - 1],
-                self.z_recv.at[i, s - 1],
-                (self.dp, (row + s) % ROWS, col),
-            )
-        self.from_partner[(i, 0, 0)] = self.remote(
-            self.blocks[i],
-            whole_block,
-            self.c_send.at[i, 0, 0],
-            self.c_recv.at[i, 0, 0],
-            self.partner,
-        )
-
-    def remote(self, src, dst, send_sem, recv_sem, device):
+
+    def own_rows(self):
+        return pl.ds(pl.multiple_of(self.row * BLOCK, BLOCK), BLOCK)
+
+    def remote(self, src, dst, send_sem, recv_sem, device, i=-1):
         copy = pltpu.make_async_remote_copy(
             src_ref=src,
             dst_ref=dst,
@@ -364,12 +361,51 @@
             device_id_type=MESH,
         )
         copy.start()
-        self.started.append(copy)
+        self.started.setdefault(i, []).append(copy)
         return copy
 
     def part(self, i, r, q):
         at = pl.multiple_of(r * BLOCK + q * PIECE, PIECE)
         return self.wholes[i].at[self.col, pl.ds(at, PIECE)]
+
+    def offer(self, i):
+        for copy in self.own[i]:
+            copy.wait()
+        row = self.row
+        self.along_z(i, row, 0, 2, (row + 2) % ROWS)
+        self.along_z(i, row, 1, 1, row + 1, row < ROWS - 1)
+        self.along_z(i, row, 2, 3, row - 1, row > 0)
+        whole_block = self.wholes[i].at[self.col, self.own_rows()]
+        self.from_partner[(i, 0, 0)] = self.remote(
+            whole_block,
+            whole_block,
+            self.c_send.at[i, 0, 0],
+            self.c_recv.at[i, 0, 0],
+            self.partner,
+            i,
+        )
+
+    def along_z(self, i, r, slot, far, to, when=None):
+        def copy():
+            ref = self.part(i, r, self.quarter)
+            return pltpu.make_async_remote_copy(
+                src_ref=ref,
+                dst_ref=ref,
+                send_sem=self.z_send.at[i, slot],
+                recv_sem=self.z_recv.at[i, far - 1],
+                device_id=(self.dp, to, self.col),
+                device_id_type=MESH,
+            )
+
+        if when is None:
+            copy().start()
+        else:
+            pl.when(when)(lambda: copy().start())
+        self.along.setdefault(i, []).append((copy, when))
+
+    def swapped(self, j):
+        self.swap_own[j].wait()
+        self.swap[j].wait_recv()
 
     def rel_onward(self):
         s_send, s_recv, base = self.rel_sems
@@ -381,8 +417,8 @@
                 self.remote(ref, ref, s_send.at[slot], s_recv.at[slot], self.partner)
             )
 
-    def rel_arrived(self, slot):
-        self.own[slot].wait()
+    def rel_arrived(self):
+        self.rel_own.wait()
         self.rel_copies[0].wait_recv()
         for copy in self.rel_copies[ROWS:]:
             copy.wait_recv()
@@ -390,7 +426,7 @@
     def hand_over(self, i, s, k, r):
         ref = self.part(i, r, self.quarter ^ k)
         self.from_partner[(i, s, k)] = self.remote(
-            ref, ref, self.c_send.at[i, s, k], self.c_recv.at[i, s, k], self.partner
+            ref, ref, self.c_send.at[i, s, k], self.c_recv.at[i, s, k], self.partner, i
         )
 
     def to_mate(self, i, s, k, slot, ref):
@@ -400,29 +436,41 @@
             self.q_send.at[i, s - 1, slot - 1],
             self.q_recv.at[i, s - 1, slot - 1],
             (quad_mate(self.dp, self.quarter, k), self.row, self.col),
-        )
+            i,
+        )
+
+    def far(self, n):
+        low, inner, high = ((3, 1, 1), (2, 3, 2), (1, 2, 3))[n - 1]
+        return jnp.where(self.row == 0, low, jnp.where(self.row == ROWS - 1, high, inner))
 
     def spread(self, i):
-        for s in range(1, ROWS):
-            self.z_copies[(i, s)].wait_recv()
-            r = (self.row - s + ROWS) % ROWS
+        row = self.row
+        for n in range(1, ROWS):
+            far = self.far(n)
+            r = (row - far + ROWS) % ROWS
             ref = self.part(i, r, self.quarter)
+            pltpu.make_async_remote_copy(
+                src_ref=ref,
+                dst_ref=ref,
+                send_sem=self.z_send.at[i, 0],
+                recv_sem=self.z_recv.at[i, far - 1],
+                device_id=self.partner,
+                device_id_type=MESH,
+            ).wait_recv()
+            if n == 3:
+                inner = (row == 1) | (row == 2)
+                self.along_z(
+                    i, r, 3, jnp.where(row == 1, 1, 3), jnp.where(row == 1, 0, 3), inner
+                )
             for k in (1, 2):
-                self.to_mate(i, s, k, k, ref)
-            self.hand_over(i, s, 0, r)
-        if i + self.AHEAD < len(self.blocks):
+                self.to_mate(i, n, k, k, ref)
+            self.hand_over(i, n, 0, r)
+        if i + self.AHEAD < len(self.wholes):
             self.offer(i + self.AHEAD)
-        self.own[i].wait()
-        self.own[i] = pltpu.make_async_copy(
-            self.own_blocks[i],
-            self.wholes[i].at[self.col, pl.ds(pl.multiple_of(self.row * BLOCK, BLOCK), BLOCK)],
-            self.local_sem.at[i],
-        )
-        self.own[i].start()
 
     def share(self, i):
         for s in range(1, ROWS):
-            r = (self.row - s + ROWS) % ROWS
+            r = (self.row - self.far(s) + ROWS) % ROWS
             onward = 1 + (i + s) % 2
             for k in (onward, 3 - onward):
                 self.q_copies[(i, s, k)].wait_recv()
@@ -433,86 +481,89 @@
     def close(self, i):
         for s in range(1, ROWS):
             self.q_copies[(i, s, 3)].wait_recv()
-            self.hand_over(i, s, 3, (self.row - s + ROWS) % ROWS)
+            self.hand_over(i, s, 3, (self.row - self.far(s) + ROWS) % ROWS)
 
     def arrived(self, i):
-        self.own[i].wait()
         for s in range(ROWS):
             for k in range(QUAD if s else 1):
                 self.from_partner[(i, s, k)].wait_recv()
 
+    def sent(self, i):
+        for copy in self.started.pop(i, ()):
+            copy.wait_send()
+        for copy, when in self.along.pop(i, ()):
+            if when is None:
+                copy().wait_send()
+            else:
+                pl.when(when)(lambda copy=copy: copy().wait_send())
+
     def finish(self):
-        for copy in self.started:
-            copy.wait_send()
-
-
-def forward_body(count, swaps, *refs):
-    blocks = refs[:count]
-    apart = refs[count : count + swaps]
-    gain_in, rel_in, onehot_ref, piece_ref = refs[count + swaps : count + swaps + 4]
-    refs = refs[count + swaps + 4 :]
-    wholes = refs[:count]
-    outs = refs[count : count + 9 + swaps + 1]
-    refs = refs[count + 9 + swaps + 1 :]
-    h2, rel_all, gains, rows_in, enc, cot, w_qkv, w_out, w_cq, w_ckv, w_co = refs[:11]
-    qkv, a1, h1, q2, kv2, a2, t8, lse1, lse2, table, load_sem, save_sem = refs[11:23]
-    own_blocks = refs[23 : 23 + count]
-    joined = (rows_in, enc, cot)
+        for i in sorted({*self.started, *self.along}):
+            self.sent(i)
+
+
+WIDTHS = (3 * HALF, HALF, HALF, 2 * HALF, HALF, 2048, 1024)
+
+
+def forward_body(*refs):
+    hidden_in, encoded, cotangent = refs[:3]
+    (s_q, s_k, s_v, s_o, x_q, x_k, x_v, x_o, f_g, f_u, f_d) = refs[3:14]
+    gain_in, rel_in, onehot_ref, piece_ref = refs[14:18]
+    outs = refs[18:36]
+    output, gu_grad, down_grad, gain_sums = refs[36:40]
+    refs = refs[40:]
+    wholes = refs[: len(WIDTHS)]
+    refs = refs[len(WIDTHS) :]
+    rel_all, gains, rows_in, enc, cot, qkv, a1, h1, q2, kv2, a2, h2, t8 = refs[:13]
+    lse1, lse2, table, dgu_all, save_sem, out_sem, stage_sem = refs[13:20]
+    col = lax.axis_index("col")
+    sources = (
+        [(w.at[:, pl.ds(128 * j, 128)], 128 * (3 * j + n)) for n, w in enumerate((s_q, s_k, s_v)) for j in range(3)],
+        [(s_o, 0)],
+        [(x_q, 0)],
+        [(x_k, 0), (x_v, HALF)],
+        [(x_o, 0)],
+        [(f_g, 0), (f_u, 1024)],
+        [(f_d, 0)],
+    )
     comm = Gathering(
-        blocks,
+        sources,
         wholes,
-        apart,
-        joined,
-        (gain_in, gains),
+        (
+            (hidden_in, col, rows_in),
+            (gain_in, None, gains),
+            (encoded, col, enc),
+            (cotangent, col, cot),
+        ),
         (rel_in, rel_all),
-        own_blocks,
-        refs[23 + count :],
+        refs[20:30],
     )
-    saving = []
-
-    class Loads(list):
-        def wait(self):
-            for copy in self:
-                copy.wait()
-
-    def load(src, dst, slot):
-        wide = src.shape[2]
-        copies = Loads()
-        for c in range(2):
-            copies.append(
-                pltpu.make_async_copy(
-                    src.at[c], dst.at[:, c * wide : (c + 1) * wide], load_sem.at[slot, c]
-                )
-            )
-            copies[-1].start()
-        return copies
+    saving = {}
 
     def save(slot, src):
         copy = pltpu.make_async_copy(src, outs[slot], save_sem.at[slot])
         copy.start()
-        saving.append(copy)
-
-    def weight(i, dst):
+        saving[slot] = copy
+
+    def weight(i):
         comm.arrived(i)
-        return load(wholes[i], dst, 3 + i)
-
-    def swapped(j, slot, ref):
-        comm.swap[j].wait_recv()
-        comm.own[count + j].wait()
-        save(slot, ref)
+        save(9 + i, wholes[i])
 
     comm.rel_onward()
     comm.spread(0)
     comm.spread(1)
-    swapped(0, 9, rows_in)
-    swapped(swaps, 9 + swaps, gains)
-    g_self = jnp.concatenate([gains[0, 0:1, :], gains[1, 0:1, :]], axis=1)
-    g_cross = jnp.concatenate([gains[0, 1:2, :], gains[1, 1:2, :]], axis=1)
+    comm.swapped(0)
+    save(14, rows_in)
+    comm.swapped(1)
+    save(16, gains)
+    g_self, g_cross, g_ffn, g_final = [
+        jnp.concatenate([gains[0, n : n + 1, :], gains[1, n : n + 1, :]], axis=1) for n in range(4)
+    ]
     comm.share(0)
     comm.spread(2)
     step = 256
     blocks_of = [slice(step * b, step * (b + 1)) for b in range(L // step)]
-    comm.rel_arrived(count + swaps + 1)
+    comm.rel_arrived()
     rel16 = jnp.concatenate([rel_all[:, :6], rel_all[:, 128:134]], axis=1).astype(bf16)
     bias = dot(rel16, onehot_ref[...], TN)
     for n in range(8):
@@ -522,13 +573,21 @@
     save(0, t8)
     comm.share(1)
     comm.close(0)
-    loading = weight(0, w_qkv)
     comm.share(2)
-    loading.wait()
+    weight(0)
+
+    def x_rows(at):
+        return jnp.concatenate([rows_in[0, at, :], rows_in[1, at, :]], axis=1).astype(f32)
+
+    def back_dot(a, i):
+        wide = wholes[i].shape[2]
+        return dot(a[:, :wide], wholes[i][0], NT) + dot(a[:, wide:], wholes[i][1], NT)
+
     for n, at in enumerate(blocks_of):
-        xb = jnp.concatenate([rows_in[0, at, :], rows_in[1, at, :]], axis=1).astype(f32)
+        xb = x_rows(at)
         n1 = (xb * rms_of(xb) * g_self).astype(bf16)
-        qkv[at, :] = dot(n1, w_qkv[...], NN).astype(bf16)
+        for c in range(2):
+            qkv[at, 3 * HALF * c : 3 * HALF * (c + 1)] = dot(n1, wholes[0][c], NN).astype(bf16)
         if n == 0:
             comm.close(1)
         if n == 1:
@@ -559,28 +618,31 @@
     lax.fori_loop(0, 2, self_heads, 0)
     comm.spread(4)
     comm.close(3)
-    loadings = [weight(1, w_out), weight(2, w_cq)]
-    swapped(1, 10, enc)
-    swapped(2, 11, cot)
+    weight(1)
+    weight(2)
+    comm.swapped(2)
+    save(15, enc)
+    comm.swapped(3)
     lax.fori_loop(2, 4, self_heads, 0)
     comm.share(4)
-    loadings.append(weight(3, w_ckv))
+    comm.spread(5)
+    weight(3)
     lax.fori_loop(4, 6, self_heads, 0)
     save(2, a1)
     save(3, lse1)
     comm.close(4)
-    comm.spread(5)
-    for copy in loadings:
-        copy.wait()
-    loading = weight(4, w_co)
-    kv2[...] = dot(jnp.concatenate([enc[0], enc[1]], axis=1), w_ckv[...], NN).astype(bf16)
+    comm.spread(6)
+    weight(4)
+    enc_rows = jnp.concatenate([enc[0], enc[1]], axis=1)
+    for c in range(2):
+        kv2[:, D * c : D * (c + 1)] = dot(enc_rows, wholes[3][c], NN).astype(bf16)
     save(6, kv2)
     for n, at in enumerate(blocks_of):
-        xb = jnp.concatenate([rows_in[0, at, :], rows_in[1, at, :]], axis=1).astype(f32)
-        h1b = xb + dot(a1[at, :], w_out[...], NT)
+        h1b = x_rows(at) + back_dot(a1[at, :], 1)
         h1[at, :] = h1b
         n2 = (h1b * rms_of(h1b) * g_cross).astype(bf16)
-        q2[at, :] = dot(n2, w_cq[...], NN).astype(bf16)
+        for c in range(2):
+            q2[at, HALF * c : HALF * (c + 1)] = dot(n2, wholes[2][c], NN).astype(bf16)
     save(4, h1)
     save(5, q2)
 
@@ -595,28 +657,117 @@
         )
         return carry
 
+    comm.share(5)
     lax.fori_loop(0, 2, cross_heads, 0)
-    comm.spread(6)
-    comm.share(5)
+    comm.share(6)
     lax.fori_loop(2, 6, cross_heads, 0)
     save(7, a2)
     save(8, lse2)
     comm.close(5)
-    loading.wait()
     for at in blocks_of:
-        h2[at, :] = h1[at, :] + dot(a2[at, :], w_co[...], NT)
-    comm.share(6)
+        h2[at, :] = h1[at, :] + back_dot(a2[at, :], 4)
+    for i in range(5):
+        comm.sent(i)
+    for copy in saving.values():
+        copy.wait()
+    comm.arrived(5)
+
+    n3t = wholes[0].at[0, :, pl.ds(0, L)]
+    e3t = wholes[0].at[1, :, pl.ds(0, L)]
+    w_gu, w_down = wholes[5], wholes[6]
+
+    def gate_rows(b, carry):
+        here = pl.ds(pl.multiple_of(b * step, step), step)
+        h2b = h2[here, :]
+        n3 = (h2b * rms_of(h2b) * g_ffn).astype(bf16)
+        n3t[:, here] = transposed(n3)
+        for c in range(4):
+            at = (c % 2) * 512
+            to = (c // 2) * 2048 + at
+            gate = dot(n3, w_gu[c // 2, :, at : at + 512], NN)
+            up = dot(n3, w_gu[c // 2, :, at + 1024 : at + 1536], NN)
+            act, slope = gelu_parts(gate)
+            qkv[here, 512 * c : 512 * (c + 1)] = (act * up).astype(bf16)
+            dgu_all[here, to : to + 512] = (up * slope).astype(bf16)
+            dgu_all[here, to + 1024 : to + 1536] = act.astype(bf16)
+        return carry
+
+    lax.fori_loop(0, 2, gate_rows, 0)
     comm.close(6)
-    comm.arrived(5)
+    lax.fori_loop(2, 4, gate_rows, 0)
     comm.arrived(6)
-    for copy in saving:
+
+    def ffn_rows(b, carry):
+        dg_ffn, dg_final = carry
+        here = pl.ds(pl.multiple_of(b * step, step), step)
+        h2b = h2[here, :]
+        h3 = h2b + back_dot(qkv[here, :2048], 6)
+        r4 = rms_of(h3)
+        a1[here, :] = (h3 * r4 * g_final).astype(bf16)
+        seen = jnp.concatenate([cot[0, here, :], cot[1, here, :]], axis=1).astype(f32)
+        dh3, more_final = norm_back_rows(h3, r4, g_final, seen)
+        e3 = dh3.astype(bf16)
+        e3t[:, here] = transposed(e3)
+        for c in range(4):
+            low = 512 * (c % 2)
+            at = (c // 2) * 2048 + low
+            dmid = dot(e3, w_down[c // 2, :, low : low + 512], NN).astype(bf16).astype(f32)
+            for to in (at, at + 1024):
+                factor = dgu_all[here, to : to + 512].astype(f32)
+                dgu_all[here, to : to + 512] = (dmid * factor).astype(bf16)
+        dn3 = back_dot(dgu_all[here, :], 5)
+        back, more_ffn = norm_back_rows(h2b, rms_of(h2b), g_ffn, dn3)
+        h2[here, :] = dh3 + back
+        return (dg_ffn + more_ffn, dg_final + more_final)
+
+    zero = jnp.zeros((1, D), f32)
+    dg_ffn, dg_final = lax.fori_loop(0, L // step, ffn_rows, (zero, zero))
+
+    def half_of(c):
+        return pl.ds(pl.multiple_of(c * HALF, 128), HALF)
+
+    leaving = comm.remote(
+        a1.at[:, half_of(1 - col)], output.at[col], out_sem.at[0], out_sem.at[1], comm.partner
+    )
+    staying = pltpu.make_async_copy(a1.at[:, half_of(col)], output.at[col], out_sem.at[2])
+    staying.start()
+    dh2_out = pltpu.make_async_copy(h2, outs[-1], out_sem.at[3])
+    dh2_out.start()
+    gain_sums[...] = jnp.zeros_like(gain_sums)
+    gain_sums[2:3, :] = dg_ffn
+    gain_sums[3:4, :] = dg_final
+    staged = {}
+
+    def stage(n, value, dst):
+        slot = n % 2
+        if slot in staged:
+            staged[slot].wait()
+        buffer = wholes[3].at[slot, :, pl.ds(0, 512)]
+        buffer[...] = value.astype(bf16)
+        staged[slot] = pltpu.make_async_copy(buffer, dst, stage_sem.at[slot])
+        staged[slot].start()
+
+    for c in range(8):
+        low = slice(512 * (c % 4), 512 * (c % 4 + 1))
+        stage(
+            c,
+            dot(n3t[...], dgu_all[:, 512 * c : 512 * (c + 1)], NN),
+            gu_grad.at[c // 4, :, low],
+        )
+    for c in range(4):
+        low = slice(512 * (c % 2), 512 * (c % 2 + 1))
+        stage(
+            c, dot(e3t[...], qkv[:, 512 * c : 512 * (c + 1)], NN), down_grad.at[c // 2, :, low]
+        )
+    for copy in staged.values():
         copy.wait()
+    staying.wait()
+    dh2_out.wait()
+    leaving.wait_recv()
     comm.finish()
 
 
-def forward(blocks, apart, gains, rel, onehot, piece, number):
-    count = len(blocks)
-    swaps = len(apart)
+def forward(args, onehot, piece, number):
     shape = jax.ShapeDtypeStruct
     saved = [
         shape((12, 8, SPAN), f32),
@@ -629,183 +780,62 @@
         shape((L, D), bf16),
         shape((6, 2, L), f32),
     ]
-    saved += [shape(x.shape, x.dtype) for x in apart] + [shape((2, 8, HALF), f32)]
-    wholes = [shape((2, D, b.shape[1]), b.dtype) for b in blocks]
+    saved += [shape((2, D, w), bf16) for w in WIDTHS[:5]]
+    saved += [shape((2, L, HALF), bf16), shape((2, LE, HALF), bf16), shape((2, 8, HALF), f32)]
+    outs = [
+        shape((2, L, HALF), bf16),
+        shape((2, D, 2048), bf16),
+        shape((2, D, 1024), bf16),
+        shape((8, D), f32),
+    ]
     dma = pltpu.SemaphoreType.DMA
     any_spec = pl.BlockSpec(memory_space=pl.ANY)
     vmem = pl.BlockSpec(memory_space=pltpu.VMEM)
-    scratch = [
+    count = len(WIDTHS)
+    scratch = [pltpu.VMEM((2, D, w), bf16) for w in WIDTHS]
+    scratch += [
         pltpu.VMEM((BUCKETS, 256), f32),
         pltpu.VMEM((2, 8, HALF), f32),
         pltpu.VMEM((2, L, HALF), bf16),
         pltpu.VMEM((2, LE, HALF), bf16),
         pltpu.VMEM((2, L, HALF), bf16),
-        pltpu.VMEM((D, 3 * D), bf16),
-        pltpu.VMEM((D, D), bf16),
-        pltpu.VMEM((D, D), bf16),
-        pltpu.VMEM((D, 2 * D), bf16),
-        pltpu.VMEM((D, D), bf16),
         pltpu.VMEM((L, 3 * D), bf16),
         pltpu.VMEM((L, D), bf16),
         pltpu.VMEM((L, D), f32),
         pltpu.VMEM((L, D), bf16),
         pltpu.VMEM((LE, 2 * D), bf16),
         pltpu.VMEM((L, D), bf16),
+        pltpu.VMEM((L, D), f32),
         pltpu.VMEM((12, 8, SPAN), f32),
         pltpu.VMEM((6, 2, L), f32),
         pltpu.VMEM((6, 2, L), f32),
         pltpu.VMEM((2, 128, SPAN), f32),
-        dma((8, 2)),
-        dma((9 + swaps + 1,)),
-    ]
-    scratch += [pltpu.VMEM(b.shape, b.dtype) for b in blocks]
-    scratch += [
-        dma((count, ROWS - 1)),
+        pltpu.VMEM((L, 4096), bf16),
+        dma((17,)),
+        dma((4,)),
+        dma((2,)),
+        dma((count, ROWS)),
         dma((count, ROWS - 1)),
         dma((count, ROWS - 1, QUAD - 1)),
         dma((count, ROWS - 1, QUAD - 1)),
         dma((count, ROWS, QUAD)),
         dma((count, ROWS, QUAD)),
-        dma((count + swaps + 2,)),
-        dma((swaps + 8,)),
-        dma((swaps + 8,)),
+        dma((count, 9)),
+        dma((11,)),
+        dma((11,)),
+        dma((5,)),
     ]
-    out = pl.pallas_call(
-        lambda *refs: forward_body(count, swaps, *refs),
-        out_shape=wholes + saved + [shape((L, D), f32)],
-        in_specs=[any_spec] * (count + swaps + 2)
-        + [vmem, pl.BlockSpec(memory_space=pltpu.SMEM)],
-        out_specs=[any_spec] * (len(wholes) + len(saved)) + [vmem],
+    return pl.pallas_call(
+        forward_body,
+        out_shape=saved + [shape((L, D), f32)] + outs,
+        in_specs=[any_spec] * 16 + [vmem, pl.BlockSpec(memory_space=pltpu.SMEM)],
+        out_specs=[any_spec] * (len(saved) + 4) + [vmem],
         scratch_shapes=scratch,
         compiler_params=pltpu.CompilerParams(
             collective_id=number, has_side_effects=True, vmem_limit_bytes=VMEM_LIMIT
         ),
         name="forward",
-    )(*blocks, *apart, gains, rel, onehot, piece)
-    return (out[:count], out[count + 9 : -1], out[count : count + 9] + out[-1:])
-
-
-def rms_of(v):
-    return lax.rsqrt(jnp.sum(v * v, axis=-1, keepdims=True) * (1.0 / D) + EPSILON)
-
-
-def norm_back_rows(v, r, gain, dn):
-    inner = jnp.sum(dn * gain * v, axis=-1, keepdims=True)
-    dv = dn * gain * r - v * (r * r * r) * (inner * (1.0 / D))
-    return (dv, jnp.sum(dn * v * r, axis=0, keepdims=True))
-
-
-def ffn_body(
-    h2_ref,
-    cot_ref,
-    gain_ref,
-    wgu_ref,
-    wd_ref,
-    out_ref,
-    dh2_ref,
-    ggu_ref,
-    gd_ref,
-    dgain_ref,
-    n3t,
-    mid_all,
-    e3t,
-    dgu_all,
-):
-    step = pl.program_id(0)
-    rows = h2_ref.shape[0]
-    here = pl.ds(pl.multiple_of(step * rows, rows), rows)
-    g_ffn = jnp.concatenate([gain_ref[0, 2:3, :], gain_ref[1, 2:3, :]], axis=1)
-    g_final = jnp.concatenate([gain_ref[0, 3:4, :], gain_ref[1, 3:4, :]], axis=1)
-    h2 = h2_ref[...]
-    r3 = rms_of(h2)
-    n3 = (h2 * r3 * g_ffn).astype(bf16)
-    n3t[:, here] = transposed(n3)
-    kept = []
-    for c in range(4):
-        at = (c % 2) * 512
-        gate = dot(n3, wgu_ref[c // 2, :, at : at + 512], NN)
-        up = dot(n3, wgu_ref[c // 2, :, at + 1024 : at + 1536], NN)
-        act, slope = gelu_parts(gate)
-        mid = (act * up).astype(bf16)
-        mid_all[here, 512 * c : 512 * (c + 1)] = mid
-        kept.append((act, up * slope))
-    h3 = h2 + dot(mid_all[here, :1024], wd_ref[0], NT) + dot(mid_all[here, 1024:], wd_ref[1], NT)
-    r4 = rms_of(h3)
-    normed = (h3 * r4 * g_final).astype(bf16)
-    out_ref[0] = normed[:, :HALF]
-    out_ref[1] = normed[:, HALF:]
-    dh3, dg_final = norm_back_rows(h3, r4, g_final, jnp.concatenate([cot_ref[0], cot_ref[1]], axis=1).astype(f32))
-    e3 = dh3.astype(bf16)
-    e3t[:, here] = transposed(e3)
-    for c in range(4):
-        at = (c // 2) * 2048 + (c % 2) * 512
-        act, slope = kept[c]
-        low = 512 * (c % 2)
-        dmid = dot(e3, wd_ref[c // 2, :, low : low + 512], NN).astype(bf16).astype(f32)
-        dgu_all[here, at : at + 512] = (dmid * slope).astype(bf16)
-        dgu_all[here, at + 1024 : at + 1536] = (dmid * act).astype(bf16)
-    dn3 = dot(dgu_all[here, :2048], wgu_ref[0], NT) + dot(dgu_all[here, 2048:], wgu_ref[1], NT)
-    back, dg_ffn = norm_back_rows(h2, r3, g_ffn, dn3)
-    dh2_ref[...] = dh3 + back
-
-    @pl.when(step == 0)
-    def _():
-        dgain_ref[...] = jnp.zeros_like(dgain_ref)
-
-    dgain_ref[2:3, :] += dg_ffn
-    dgain_ref[3:4, :] += dg_final
-
-    @pl.when(step == pl.num_programs(0) - 1)
-    def _():
-        for c in range(8):
-            span = slice(512 * c, 512 * (c + 1))
-            low = slice(512 * (c % 4), 512 * (c % 4 + 1))
-            ggu_ref[c // 4, :, low] = dot(n3t[...], dgu_all[:, span], NN).astype(bf16)
-        for c in range(4):
-            span = slice(512 * c, 512 * (c + 1))
-            low = slice(512 * (c % 2), 512 * (c % 2 + 1))
-            gd_ref[c // 2, :, low] = dot(e3t[...], mid_all[:, span], NN).astype(bf16)
-
-
-def feed_forward(h2, cot, gains, wgu, wd):
-    rows = 256
-    def whole(*shape):
-        return pl.BlockSpec(shape, lambda i: (0,) * len(shape), pipeline_mode=pl.Buffered(1))
-
-    block = pl.BlockSpec((rows, D), lambda i: (i, 0))
-    return pl.pallas_call(
-        ffn_body,
-        grid=(L // rows,),
-        in_specs=[
-            block,
-            pl.BlockSpec((2, rows, HALF), lambda i: (0, i, 0)),
-            whole(2, 8, HALF),
-            whole(2, D, 2048),
-            whole(2, D, 1024),
-        ],
-        out_specs=[
-            pl.BlockSpec((2, rows, HALF), lambda i: (0, i, 0)),
-            block,
-            whole(2, D, 2048),
-            whole(2, D, 1024),
-            whole(8, D),
-        ],
-        out_shape=[
-            jax.ShapeDtypeStruct((2, L, HALF), bf16),
-            jax.ShapeDtypeStruct((L, D), f32),
-            jax.ShapeDtypeStruct((2, D, 2048), bf16),
-            jax.ShapeDtypeStruct((2, D, 1024), bf16),
-            jax.ShapeDtypeStruct((8, D), f32),
-        ],
-        scratch_shapes=[
-            pltpu.VMEM((D, L), bf16),
-            pltpu.VMEM((L, 2048), bf16),
-            pltpu.VMEM((D, L), bf16),
-            pltpu.VMEM((L, 4096), bf16),
-        ],
-        compiler_params=pltpu.CompilerParams(vmem_limit_bytes=VMEM_LIMIT),
-        name="feed_forward",
-    )(h2, cot, gains, wgu, wd)
+    )(*args, onehot, piece)
 
 
 class Summing:
@@ -845,7 +875,59 @@
     def offer(self, i, src):
         self.send(i, 0, src, self.pair[i], self.partner)
 
+    def z_first1(self, i, own):
+        self.pending[(i, 0)].wait_recv()
+        pair = self.pair[i]
+        for r in range(ROWS):
+            pair[r] = pair[r] + own(r)
+        for s in range(1, ROWS):
+            to = (self.row + s) % ROWS
+            self.send(i, 6 + s, pair.at[to], self.third[i].at[s - 1], (self.dp, to, self.col))
+
+    def z_first2(self, i):
+        for s in range(1, ROWS):
+            self.pending[(i, 6 + s)].wait_recv()
+        block = self.pair[i].at[self.row]
+        third = self.third[i]
+        for q in range(QUAD):
+            total = block[q].astype(f32)
+            for s in range(1, ROWS):
+                total = total + third[s - 1, q].astype(f32)
+            block[q] = total.astype(bf16)
+        wide = self.widths[i] // 2
+        for h in range(2):
+            k = 1 + h
+            for j, q in enumerate((self.quarter ^ k, self.quarter ^ 3)):
+                self.send(
+                    i,
+                    1 + 2 * h + j,
+                    block.at[q, :, pl.ds(wide * h, wide)],
+                    self.first[i].at[h, j],
+                    self.mate(k),
+                )
+
+    def z_first3(self, i):
+        block, first = self.pair[i].at[self.row], self.first[i]
+        wide = self.widths[i] // 2
+        for h in range(2):
+            k = 1 + h
+            for j in range(2):
+                self.pending[(i, 1 + 2 * h + j)].wait_recv()
+            span = pl.ds(wide * h, wide)
+            first[h, 1] = first[h, 1] + block[self.quarter ^ 3 ^ k, :, span]
+            self.send(i, 5 + h, first.at[h, 1], self.second[i].at[h], self.mate(3 ^ k))
+            first[h, 0] = first[h, 0] + block[self.quarter, :, span]
+
+    def z_first4(self, i):
+        wide = self.widths[i] // 2
+        for h in range(2):
+            self.pending[(i, 5 + h)].wait_recv()
+            self.final[i][:, wide * h : wide * (h + 1)] = self.second[i][h] + self.first[i][h, 0]
+        self.give_back(i)
+
     def stage1(self, i, own):
+        if i in Z_FIRST:
+            return self.z_first1(i, own)
         self.pending[(i, 0)].wait_recv()
         pair = self.pair[i]
         for r in range(ROWS):
@@ -862,6 +944,8 @@
                     )
 
     def stage2(self, i):
+        if i in Z_FIRST:
+            return self.z_first2(i)
         first, pair = self.first[i], self.pair[i]
         for h in range(2):
             k = 1 if h == 0 else 2
@@ -880,6 +964,8 @@
                 first[r, 0] = first[r, 0] + pair[r, self.quarter]
 
     def stage3(self, i):
+        if i in Z_FIRST:
+            return self.z_first3(i)
         second = self.second[i]
         for h in range(2):
             self.pending[(i, 5 + h)].wait_recv()
@@ -890,12 +976,17 @@
             self.send(i, 6 + s, second.at[to], self.third[i].at[s - 1], (self.dp, to, self.col))
 
     def stage4(self, i):
+        if i in Z_FIRST:
+            return self.z_first4(i)
         for s in range(1, ROWS):
             self.pending[(i, 6 + s)].wait_recv()
         total = self.second[i][self.row].astype(f32)
         for s in range(1, ROWS):
             total = total + self.third[i][s - 1].astype(f32)
         self.final[i][...] = total.astype(bf16)
+        self.give_back(i)
+
+    def give_back(self, i):
         there = self.outs[i].at[self.quarter]
         for k in (1, 2):
             self.send(i, 9 + k, self.final[i], there, self.mate(k))
@@ -922,6 +1013,7 @@
 
 CHUNKS = (1024, 1024, 1024, HALF, HALF, 2 * HALF, HALF, HALF, HALF, HALF)
 (F0, F1, F2, CO, CQ, CKV, SO, QA, QB, QC) = range(10)
+Z_FIRST = (F0,)
 SMALL = (16, 896)
 
 
@@ -946,17 +1038,16 @@
         w_cq_in,
         w_ckv_in,
         w_co_in,
-        made,
         gains,
         ffn_gains,
         onehot_ref,
         piece_ref,
-    ) = refs[:24]
+    ) = refs[:23]
     count = len(CHUNKS)
-    output, hidden_grad, enc_grad = refs[24:27]
-    sums = refs[27 : 27 + count]
-    small_out = refs[27 + count]
-    refs = refs[28 + count :]
+    hidden_grad, enc_grad = refs[23:25]
+    sums = refs[25 : 25 + count]
+    small_out = refs[25 + count]
+    refs = refs[26 + count :]
     pair = refs[:count]
     first = refs[count : 2 * count]
     second = refs[2 * count : 3 * count]
@@ -1002,10 +1093,6 @@
             ],
         )
 
-    bouncing = load(0, (made.at[col], dmixed.at[:, :HALF]))
-    ex_out = comm.remote(
-        made.at[1 - col], output.at[col], ex_send.at[0], ex_recv.at[0], partner
-    )
     comm.offer(F0, g_gu.at[1 - col, :, :, :, pl.ds(0, 1024)])
     comm.offer(F1, g_gu.at[1 - col, :, :, :, pl.ds(1024, 1024)])
     comm.offer(F2, g_down.at[1 - col])
@@ -1044,14 +1131,10 @@
         slot = i % 2
         return lambda r: gr_qkv[slot * 4 + r, :, :, pl.ds(0, 1024)]
 
-    wait(bouncing)
-    keep_out = pltpu.make_async_copy(dmixed.at[:, :HALF], output.at[col], ex_local.at[0])
-    keep_out.start()
     wait(l_total)
     for at in blocks_of:
         turned[:, at] = transposed(total[at, :])
     wait(l_co)
-    keep_out.wait()
     for at in blocks_of:
         dmixed[at, :] = dot(total[at, :].astype(bf16), w_big[:, 2 * D :], NN).astype(bf16)
     wait(l_a2)
@@ -1085,7 +1168,6 @@
     comm.stage1(F1, own_loaded(1))
     l_own.append(own_ffn(2))
     lax.fori_loop(2, 4, cross_heads, 0)
-    comm.stage2(F0)
     wait(l_own[2])
     comm.stage1(F2, own_loaded(2))
     comm.stage1(CO, own_of(gr_co))
@@ -1109,7 +1191,6 @@
         put(gr_ckv.at[c], dot(enct, qkv[:LE, D + D * c : D + D * (c + 1)], NN))
     comm.offer(CKV, gr_ckv.at[1 - col])
     comm.stage2(F2)
-    comm.stage3(F0)
     wait(l_ckv)
     back = dot(qkv[:LE, D:], w_big[:, : 2 * D], NT)
     eg[0] = back[:, :HALF]
@@ -1195,7 +1276,7 @@
     self_heads(0)
     comm.stage1(SO, own_of(gr_out))
     comm.stage2(CQ)
-    comm.stage4(F0)
+    comm.stage2(F0)
     self_heads(3)
     comm.stage2(CKV)
     comm.stage4(F1)
@@ -1207,12 +1288,13 @@
     comm.stage3(CKV)
     comm.stage4(F2)
     comm.stage4(CO)
-    comm.stage5(F0)
+    comm.stage3(F0)
     self_heads(4)
     comm.stage2(QA)
     comm.stage3(SO)
     comm.stage4(CQ)
     comm.stage5(F1)
+    comm.stage4(F0)
     grads_of(1)
     self_heads(2)
     comm.stage1(QB, own_qkv(1))
@@ -1226,6 +1308,7 @@
     comm.stage4(SO)
     comm.stage5(CQ)
     comm.stage5(CKV)
+    comm.stage5(F0)
     grads_of(2)
     comm.stage3(QB)
 
@@ -1302,7 +1385,6 @@
         passing[2 + s].wait_recv()
     small_out[...] = (small[6] + small[7]) + (small[8] + small[9])
     keep_eg.wait()
-    ex_out.wait_recv()
     ex_eg.wait_recv()
     for copy in leaving:
         copy.wait_recv()
@@ -1317,9 +1399,15 @@
     count = len(CHUNKS)
     quarters = (ROWS, QUAD, PIECE)
     scratch = [pltpu.VMEM(quarters + (w,), bf16) for w in CHUNKS]
-    scratch += [pltpu.VMEM((ROWS, 2, PIECE, w), bf16) for w in CHUNKS]
-    scratch += [pltpu.VMEM((ROWS, PIECE, w), bf16) for w in CHUNKS]
-    scratch += [pltpu.VMEM((ROWS - 1, PIECE, w), bf16) for w in CHUNKS]
+    for normal, z_first in (
+        (lambda w: (ROWS, 2, PIECE, w), lambda w: (2, 2, PIECE, w // 2)),
+        (lambda w: (ROWS, PIECE, w), lambda w: (2, PIECE, w // 2)),
+        (lambda w: (ROWS - 1, PIECE, w), lambda w: (ROWS - 1, QUAD, PIECE, w)),
+    ):
+        scratch += [
+            pltpu.VMEM((z_first if i in Z_FIRST else normal)(w), bf16)
+            for i, w in enumerate(CHUNKS)
+        ]
     scratch += [pltpu.VMEM((PIECE, w), bf16) for w in CHUNKS]
     scratch += [
         pltpu.VMEM((2,) + quarters + (HALF,), bf16),
@@ -1360,33 +1448,22 @@
     out = pl.pallas_call(
         backward_body,
         out_shape=[
-            shape((2, L, HALF), bf16),
             shape((2, L, HALF), f32),
             shape((2, LE, HALF), f32),
         ]
         + [shape((QUAD, PIECE, w), bf16) for w in CHUNKS]
         + [shape(SMALL, f32)],
-        in_specs=[any_spec] * 20
+        in_specs=[any_spec] * 19
         + [vmem] * 3
         + [pl.BlockSpec(memory_space=pltpu.SMEM)],
-        out_specs=[any_spec] * (3 + count) + [vmem],
+        out_specs=[any_spec] * (2 + count) + [vmem],
         scratch_shapes=scratch,
         compiler_params=pltpu.CompilerParams(
             collective_id=number, has_side_effects=True, vmem_limit_bytes=VMEM_LIMIT
         ),
         name="backward",
     )(*args, onehot, piece)
-    return (out[:3], [o.reshape(BLOCK, o.shape[2]) for o in out[3:-1]], out[-1])
-
-
-def inverse_rms(v):
-    return lax.rsqrt(jnp.mean(v * v, axis=-1, keepdims=True) + EPSILON)
-
-
-def norm_backward(v, r, gain, dn):
-    inner = jnp.sum(dn * gain * v, axis=-1, keepdims=True)
-    dv = dn * gain * r - v * (r * r * r) * (inner / D)
-    return (dv, jnp.sum(dn * v * r, axis=0))
+    return (out[:2], [o.reshape(BLOCK, o.shape[2]) for o in out[2:-1]], out[-1])
 
 
 def gelu_parts(t):
@@ -1426,17 +1503,6 @@
 ):
     col = lax.axis_index("col")
     row = lax.axis_index("row")
-    blocks = (
-        jnp.stack(
-            [w.reshape(BLOCK, 3, 128) for w in (self_query, self_key, self_value)], axis=2
-        ).reshape(BLOCK, 3 * HALF),
-        self_out.T,
-        cross_query,
-        jnp.concatenate([cross_key, cross_value], axis=1),
-        cross_out.T,
-        jnp.concatenate([ffn_gate, ffn_up], axis=1),
-        ffn_down.T,
-    )
     gain_block = jnp.stack([gain_self, gain_cross, gain_ffn, gain_final])
     gain_block = jnp.concatenate([gain_block, jnp.zeros_like(gain_block)])
     rel_block = jnp.pad(rel_weight.astype(f32), ((0, 0), (0, 122)))
@@ -1445,19 +1511,33 @@
     starts = lax.dynamic_index_in_dim(piece_start, col, 0, keepdims=False)
     lengths = lax.dynamic_index_in_dim(image_piece_lengths, col, 0, keepdims=False)
     piece = jnp.concatenate([starts, starts + lengths])
-    wholes, (x, enc, cot, gains), saved = forward(
-        blocks,
-        (hidden_in, encoded, cotangent),
-        gain_block,
-        rel_block,
+    out = forward(
+        (
+            hidden_in,
+            encoded,
+            cotangent,
+            self_query,
+            self_key,
+            self_value,
+            self_out.T,
+            cross_query,
+            cross_key,
+            cross_value,
+            cross_out.T,
+            ffn_gate,
+            ffn_up,
+            ffn_down.T,
+            gain_block,
+            rel_block,
+        ),
         onehot,
         piece,
         0,
     )
-    t8, qkv, a1, lse1, h1, q2, kv2, a2, lse2, h2 = saved
-    made, dh2, gr_gu, gr_down, ffn_gains = feed_forward(h2, cot, gains, wholes[5], wholes[6])
+    t8, qkv, a1, lse1, h1, q2, kv2, a2, lse2 = out[:9]
+    x, enc, gains, dh2, output, gr_gu, gr_down, ffn_gains = out[14:]
     cut = (2, ROWS, QUAD, PIECE)
-    (output, hidden_grad, enc_grad), grads, small = backward(
+    (hidden_grad, enc_grad), grads, small = backward(
         (
             dh2,
             gr_gu.reshape(cut + (2048,)),
@@ -1473,8 +1553,7 @@
             lse2,
             x,
             enc,
-            *wholes[:5],
-            made,
+            *out[9:14],
             gains,
             ffn_gains,
         ),

time: 326 us -> 294 us (0.902)
  Pallas kernels: 292 us -> 264 us
    pallas_call x3 -> x2, Pallas kernels: 292 us -> 264 us  [the longest x1 142 us: forward(): pl.pallas_call(forward_body, out_shape=saved + [shape((L, D), f32)] + out...]
    another operation x4 -> x0, local copies, waits for them, and re-layouts: 3.48 us -> none  [body(): jnp.stack([w.reshape(BLOCK, 3, 128) for w in (self_query, self_key, self_...]
where the time goes in v1:
time: 294 us; the launch traced here: 289 us
  Pallas kernels  264 us (90%)
  local copies, waits for them, and re-layouts  13 us (4%)
  other arithmetic  10.6 us (4%)
    pallas_call x1, Pallas kernels, forward(): pl.pallas_call(forward_body, out_shape=saved + [shape((L, D), f32)] + out...  142 us
    pallas_call x1, Pallas kernels, backward(): pl.pallas_call(backward_body, out_shape=[shape((2, L, HALF), f32), shape(...  122 us

profile of v1, /device:TPU:0, one launch (start us, length us, event | category | flops | bytes accessed | tf_op | source)
XLA Modules:
  0.0 288.9 jit_solution(4974130923634933533)
XLA Ops:
  0.7 0.7 stack.12
  1.3 0.7 stack.13
  2.0 0.7 stack.14
  2.7 0.7 stack.15
  3.4 0.6 concatenate.15.refs_14_
  4.0 1.3 pad_convert_fusion.refs_15_
  5.3 0.8 rev.3
  6.1 0.7 fusion.refs_16_.refs_21_
  6.7 0.7 fusion.3
  7.4 0.6 pad_add_fusion.refs_17_.refs_22_
  8.0 142.4 %forward.1 = (f32[12,8,1536]{2,1,0:T(8,128)}, bf16[1024,2304]{1,0:T(8,128)(2,1)}, bf16[1024,768]{1,0:T(8,128)(2,1)}, f32[6,2,1024]{2,1,0:T(2,128)}, f32[1024,768...) custom-call(bf16[2,1024,384]{2,1,0:T(8,128)(2,1)} %refs_0_.1, ...), custom_call_target="tpu_custom_call" | custom-call | tf_op jit(solution)/shard_map/forward/pallas_call | solution.py:828
  150.4 122.0 %backward.1 = (f32[2,1024,384]{2,1,0:T(8,128)}, f32[2,256,384]{2,1,0:T(8,128)}, bf16[4,48,1024]{2,1,0:T(8,128)(2,1)}, bf16[4,48,1024]{2,1,0:T(8,128)(2,1)}, bf16...) custom-call(f32[1024,768]{1,0:T(8,128)} %get-tuple-element.55.refs_0, ...), custom_call_target="tpu_custom_call" | custom-call | tf_op jit(solution)/shard_map/backward/pallas_call | solution.py:1448
  272.5 0.0 copy-start.9
  272.5 0.0 copy-start.10
  272.5 1.8 bitcast_convert_fusion.3
  274.3 0.0 copy-done.9
  274.3 0.0 copy-done.10
  274.3 0.1 bitcast_convert_fusion.5
  274.4 0.0 copy-start.7
  274.4 0.0 copy-start.8
  274.4 0.0 copy-start.6
  274.5 0.7 pad_maximum_fusion
  275.2 0.7 pad_maximum_fusion.1
  275.9 0.7 pad_maximum_fusion.2
  276.7 0.0 copy-start.5
  276.7 0.0 copy-done.7
  276.7 0.0 copy-done.8
  276.7 0.9 convert_bitcast_fusion.1
  277.6 0.8 dynamic-slice_bitcast_fusion
  278.3 0.7 copy.41
  279.0 0.0 copy-done.6
  279.0 0.0 copy-start.3
  279.0 0.0 copy-start.4
  279.0 0.1 bitcast_convert_fusion.2
  279.1 0.9 fusion.5
  279.9 0.0 copy-done.5
  279.9 0.0 copy-start.1
  279.9 1.0 bitcast_convert_fusion.1
  280.9 0.0 copy-done.3
  280.9 0.0 copy-done.4
  280.9 1.4 convert_bitcast_fusion
  282.3 0.8 slice.63
  283.0 0.7 dynamic-slice_reduce_fusion
  283.7 0.0 copy-done.1
  283.7 0.0 copy-start
  283.7 1.1 copy.45
  284.9 1.3 copy-done
  286.2 0.0 copy-start.2
  286.2 1.7 copy.46
  287.8 0.0 copy-done.2
  287.9 0.9 copy.47
  (4 shorter events, 0.1 us)
Async XLA Ops:
  272.5 1.8 copy-start.9
  272.5 1.8 copy-start.10
  274.4 2.3 copy-start.7
  274.4 2.3 copy-start.8
  274.4 4.6 %copy-start.6 = (bf16[4,48,768]{2,1,0:T(8,128)(2,1)S(1)}, bf16[4,48,768]{2,1,0:T(8,128)(2,1)}, u32[]{:S(2)}) copy-start(bf16[4,48,768]{2,1,0:T(8,128)(2,1)} %get-tuple-element.84) | copy-start | bytes 884740
  276.7 3.3 %copy-start.5 = (bf16[4,48,1024]{2,1,0:T(8,128)(2,1)S(1)}, bf16[4,48,1024]{2,1,0:T(8,128)(2,1)}, u32[]{:S(2)}) copy-start(bf16[4,48,1024]{2,1,0:T(8,128)(2,1)} %get-tuple-element.86) | copy-start | bytes 1179652
  279.0 1.9 copy-start.3
  279.0 1.9 copy-start.4
  279.9 3.8 %copy-start.1 = (bf16[2,1024,384]{2,1,0:T(8,128)(2,1)S(1)}, bf16[2,1024,384]{2,1,0:T(8,128)(2,1)}, u32[]{:S(2)}) copy-start(bf16[2,1024,384]{2,1,0:T(8,128)(2,1)} %get-tuple-element.152) | copy-start | bytes 4718596
  283.7 2.5 copy-start
  286.2 1.7 copy-start.2

commit v2 on v1

--- a/solution.py
+++ b/solution.py
@@ -273,10 +273,11 @@
 
 
 class Gathering:
-    AHEAD = 3
+    AHEAD = 5
 
     def __init__(self, sources, wholes, swaps, rel_pair, sems):
         self.wholes = wholes
+        self.items = ITEMS
         self.dp, self.quarter, self.row, self.col = place()
         self.partner = (self.dp, self.row, 1 - self.col)
         (
@@ -300,7 +301,7 @@
             for n, (src, to) in enumerate(parts):
                 copy = pltpu.make_async_copy(
                     src,
-                    wholes[i].at[col, self.own_rows(), pl.ds(to, src.shape[1])],
+                    self.lanes_of(i, self.own_rows(), to, src.shape[1]),
                     own_sem.at[i, n],
                 )
                 copy.start()
@@ -348,6 +349,10 @@
         for i in range(self.AHEAD):
             self.offer(i)
 
+    def lanes_of(self, i, rows, offset=0, width=None):
+        array, low, wide = self.items[i]
+        return self.wholes[array].at[self.col, rows, pl.ds(low + offset, width or wide)]
+
     def own_rows(self):
         return pl.ds(pl.multiple_of(self.row * BLOCK, BLOCK), BLOCK)
 
@@ -366,7 +371,7 @@
 
     def part(self, i, r, q):
         at = pl.multiple_of(r * BLOCK + q * PIECE, PIECE)
-        return self.wholes[i].at[self.col, pl.ds(at, PIECE)]
+        return self.lanes_of(i, pl.ds(at, PIECE))
 
     def offer(self, i):
         for copy in self.own[i]:
@@ -375,7 +380,7 @@
         self.along_z(i, row, 0, 2, (row + 2) % ROWS)
         self.along_z(i, row, 1, 1, row + 1, row < ROWS - 1)
         self.along_z(i, row, 2, 3, row - 1, row > 0)
-        whole_block = self.wholes[i].at[self.col, self.own_rows()]
+        whole_block = self.lanes_of(i, self.own_rows())
         self.from_partner[(i, 0, 0)] = self.remote(
             whole_block,
             whole_block,
@@ -465,7 +470,7 @@
             for k in (1, 2):
                 self.to_mate(i, n, k, k, ref)
             self.hand_over(i, n, 0, r)
-        if i + self.AHEAD < len(self.wholes):
+        if i + self.AHEAD < len(self.items):
             self.offer(i + self.AHEAD)
 
     def share(self, i):
@@ -503,6 +508,9 @@
 
 
 WIDTHS = (3 * HALF, HALF, HALF, 2 * HALF, HALF, 2048, 1024)
+ITEMS = tuple((0, HALF * j, HALF) for j in range(3)) + tuple(
+    (i, 0, w) for i, w in enumerate(WIDTHS) if i
+)
 
 
 def forward_body(*refs):
@@ -518,7 +526,10 @@
     lse1, lse2, table, dgu_all, save_sem, out_sem, stage_sem = refs[13:20]
     col = lax.axis_index("col")
     sources = (
-        [(w.at[:, pl.ds(128 * j, 128)], 128 * (3 * j + n)) for n, w in enumerate((s_q, s_k, s_v)) for j in range(3)],
+        *[
+            [(w.at[:, pl.ds(128 * j, 128)], 128 * n) for n, w in enumerate((s_q, s_k, s_v))]
+            for j in range(3)
+        ],
         [(s_o, 0)],
         [(x_q, 0)],
         [(x_k, 0), (x_v, HALF)],
@@ -546,12 +557,16 @@
         saving[slot] = copy
 
     def weight(i):
-        comm.arrived(i)
+        for n, item in enumerate(ITEMS):
+            if item[0] == i:
+                comm.arrived(n)
         save(9 + i, wholes[i])
 
-    comm.rel_onward()
     comm.spread(0)
     comm.spread(1)
+    comm.rel_onward()
+    comm.spread(2)
+    comm.share(0)
     comm.swapped(0)
     save(14, rows_in)
     comm.swapped(1)
@@ -559,8 +574,9 @@
     g_self, g_cross, g_ffn, g_final = [
         jnp.concatenate([gains[0, n : n + 1, :], gains[1, n : n + 1, :]], axis=1) for n in range(4)
     ]
-    comm.share(0)
-    comm.spread(2)
+    comm.share(1)
+    comm.share(2)
+    comm.spread(3)
     step = 256
     blocks_of = [slice(step * b, step * (b + 1)) for b in range(L // step)]
     comm.rel_arrived()
@@ -571,9 +587,11 @@
         for h in range(12):
             t8[h, n : n + 1, :] = moved[h : h + 1]
     save(0, t8)
-    comm.share(1)
     comm.close(0)
-    comm.share(2)
+    comm.close(1)
+    comm.spread(4)
+    comm.close(2)
+    comm.share(3)
     weight(0)
 
     def x_rows(at):
@@ -589,13 +607,14 @@
         for c in range(2):
             qkv[at, 3 * HALF * c : 3 * HALF * (c + 1)] = dot(n1, wholes[0][c], NN).astype(bf16)
         if n == 0:
-            comm.close(1)
+            comm.close(3)
+            comm.share(4)
         if n == 1:
-            comm.spread(3)
+            comm.spread(5)
         if n == 2:
-            comm.close(2)
+            comm.close(4)
         if n == 3:
-            comm.share(3)
+            comm.share(5)
     save(1, qkv)
 
     def lane(block):
@@ -616,22 +635,22 @@
         return carry
 
     lax.fori_loop(0, 2, self_heads, 0)
-    comm.spread(4)
-    comm.close(3)
+    comm.spread(6)
+    comm.close(5)
     weight(1)
     weight(2)
     comm.swapped(2)
     save(15, enc)
     comm.swapped(3)
     lax.fori_loop(2, 4, self_heads, 0)
-    comm.share(4)
-    comm.spread(5)
+    comm.share(6)
+    comm.spread(7)
     weight(3)
     lax.fori_loop(4, 6, self_heads, 0)
     save(2, a1)
     save(3, lse1)
-    comm.close(4)
-    comm.spread(6)
+    comm.close(6)
+    comm.spread(8)
     weight(4)
     enc_rows = jnp.concatenate([enc[0], enc[1]], axis=1)
     for c in range(2):
@@ -657,20 +676,20 @@
         )
         return carry
 
-    comm.share(5)
+    comm.share(7)
     lax.fori_loop(0, 2, cross_heads, 0)
-    comm.share(6)
+    comm.share(8)
     lax.fori_loop(2, 6, cross_heads, 0)
     save(7, a2)
     save(8, lse2)
-    comm.close(5)
+    comm.close(7)
     for at in blocks_of:
         h2[at, :] = h1[at, :] + back_dot(a2[at, :], 4)
-    for i in range(5):
+    for i in range(7):
         comm.sent(i)
     for copy in saving.values():
         copy.wait()
-    comm.arrived(5)
+    comm.arrived(7)
 
     n3t = wholes[0].at[0, :, pl.ds(0, L)]
     e3t = wholes[0].at[1, :, pl.ds(0, L)]
@@ -693,9 +712,9 @@
         return carry
 
     lax.fori_loop(0, 2, gate_rows, 0)
-    comm.close(6)
+    comm.close(8)
     lax.fori_loop(2, 4, gate_rows, 0)
-    comm.arrived(6)
+    comm.arrived(8)
 
     def ffn_rows(b, carry):
         dg_ffn, dg_final = carry
@@ -791,7 +810,7 @@
     dma = pltpu.SemaphoreType.DMA
     any_spec = pl.BlockSpec(memory_space=pl.ANY)
     vmem = pl.BlockSpec(memory_space=pltpu.VMEM)
-    count = len(WIDTHS)
+    count = len(ITEMS)
     scratch = [pltpu.VMEM((2, D, w), bf16) for w in WIDTHS]
     scratch += [
         pltpu.VMEM((BUCKETS, 256), f32),
@@ -820,7 +839,7 @@
         dma((count, ROWS - 1, QUAD - 1)),
         dma((count, ROWS, QUAD)),
         dma((count, ROWS, QUAD)),
-        dma((count, 9)),
+        dma((count, 3)),
         dma((11,)),
         dma((11,)),
         dma((5,)),
@@ -1503,8 +1522,9 @@
 ):
     col = lax.axis_index("col")
     row = lax.axis_index("row")
-    gain_block = jnp.stack([gain_self, gain_cross, gain_ffn, gain_final])
-    gain_block = jnp.concatenate([gain_block, jnp.zeros_like(gain_block)])
+    gain_block = jnp.tile(
+        jnp.concatenate([gain_self, gain_cross, gain_ffn, gain_final]).reshape(4, HALF), (2, 1)
+    )
     rel_block = jnp.pad(rel_weight.astype(f32), ((0, 0), (0, 122)))
     turned_table = bucket_table[:SPAN][::-1]
     onehot = (turned_table[None, :] == jnp.arange(BUCKETS, dtype=jnp.int32)[:, None]).astype(bf16)

time: 294 us -> 288 us (0.980)
  Pallas kernels: 264 us -> 260 us
where the time goes in v2:
time: 288 us; the launch traced here: 283 us
  Pallas kernels  260 us (90%)
  other arithmetic  11.3 us (4%)
  local copies, waits for them, and re-layouts  10.2 us (4%)
    pallas_call x1, Pallas kernels, forward(): pl.pallas_call(forward_body, out_shape=saved + [shape((L, D), f32)] + out...  140 us
    pallas_call x1, Pallas kernels, backward(): pl.pallas_call(backward_body, out_shape=[shape((2, L, HALF), f32), shape(...  120 us

profile of v2, /device:TPU:0, one launch (start us, length us, event | category | flops | bytes accessed | tf_op | source)
XLA Modules:
  0.0 282.6 jit_solution(1417893345279480355)
XLA Ops:
  0.7 0.7 pad_maximum_fusion.3
  1.4 0.6 tile.12.refs_14_
  2.0 1.3 pad_convert_fusion.refs_15_
  3.3 0.8 rev.3
  4.1 0.7 fusion.refs_16_.refs_21_
  4.7 0.7 fusion.3
  5.4 0.6 pad_add_fusion.refs_17_.refs_22_
  6.0 140.4 %forward.1 = (f32[12,8,1536]{2,1,0:T(8,128)}, bf16[1024,2304]{1,0:T(8,128)(2,1)}, bf16[1024,768]{1,0:T(8,128)(2,1)}, f32[6,2,1024]{2,1,0:T(2,128)}, f32[1024,768...) custom-call(bf16[2,1024,384]{2,1,0:T(8,128)(2,1)} %refs_0_.1, ...), custom_call_target="tpu_custom_call" | custom-call | tf_op jit(solution)/shard_map/forward/pallas_call | solution.py:847
  146.4 119.7 %backward.1 = (f32[2,1024,384]{2,1,0:T(8,128)}, f32[2,256,384]{2,1,0:T(8,128)}, bf16[4,48,1024]{2,1,0:T(8,128)(2,1)}, bf16[4,48,1024]{2,1,0:T(8,128)(2,1)}, bf16...) custom-call(f32[1024,768]{1,0:T(8,128)} %get-tuple-element.55.refs_0, ...), custom_call_target="tpu_custom_call" | custom-call | tf_op jit(solution)/shard_map/backward/pallas_call | solution.py:1467
  266.1 0.0 copy-start.9
  266.1 0.0 copy-start.10
  266.1 1.8 bitcast_convert_fusion.3
  267.9 0.0 copy-done.9
  267.9 0.0 copy-done.10
  267.9 0.1 bitcast_convert_fusion.5
  268.0 0.0 copy-start.7
  268.0 0.0 copy-start.8
  268.1 0.0 copy-start.6
  268.1 0.7 pad_maximum_fusion
  268.8 0.7 pad_maximum_fusion.1
  269.6 0.7 pad_maximum_fusion.2
  270.3 0.0 copy-start.5
  270.3 0.0 copy-done.7
  270.3 0.0 copy-done.8
  270.3 0.9 convert_bitcast_fusion.1
  271.2 0.8 dynamic-slice_bitcast_fusion
  272.0 0.7 copy.41
  272.6 0.0 copy-done.6
  272.6 0.0 copy-start.3
  272.6 0.0 copy-start.4
  272.6 0.1 bitcast_convert_fusion.2
  272.7 0.9 fusion.5
  273.6 0.0 copy-done.5
  273.6 0.0 copy-start.1
  273.6 1.0 bitcast_convert_fusion.1
  274.5 0.0 copy-done.3
  274.5 0.0 copy-done.4
  274.6 1.4 convert_bitcast_fusion
  275.9 0.8 slice.63
  276.7 0.7 dynamic-slice_reduce_fusion
  277.4 0.0 copy-done.1
  277.4 0.0 copy-start
  277.4 1.1 copy.45
  278.5 1.3 copy-done
  279.8 0.0 copy-start.2
  279.8 1.7 copy.46
  281.5 0.0 copy-done.2
  281.5 0.9 copy.47
  (5 shorter events, 0.1 us)
Async XLA Ops:
  266.1 1.8 copy-start.9
  266.1 1.8 copy-start.10
  268.0 2.3 copy-start.7
  268.0 2.3 copy-start.8
  268.1 4.6 %copy-start.6 = (bf16[4,48,768]{2,1,0:T(8,128)(2,1)S(1)}, bf16[4,48,768]{2,1,0:T(8,128)(2,1)}, u32[]{:S(2)}) copy-start(bf16[4,48,768]{2,1,0:T(8,128)(2,1)} %get-tuple-element.84) | copy-start | bytes 884740
  270.3 3.3 %copy-start.5 = (bf16[4,48,1024]{2,1,0:T(8,128)(2,1)S(1)}, bf16[4,48,1024]{2,1,0:T(8,128)(2,1)}, u32[]{:S(2)}) copy-start(bf16[4,48,1024]{2,1,0:T(8,128)(2,1)} %get-tuple-element.86) | copy-start | bytes 1179652
  272.6 1.9 copy-start.3
  272.6 1.9 copy-start.4
  273.6 3.8 %copy-start.1 = (bf16[2,1024,384]{2,1,0:T(8,128)(2,1)S(1)}, bf16[2,1024,384]{2,1,0:T(8,128)(2,1)}, u32[]{:S(2)}) copy-start(bf16[2,1024,384]{2,1,0:T(8,128)(2,1)} %get-tuple-element.152) | copy-start | bytes 4718596
  277.4 2.5 copy-start
  279.8 1.7 copy-start.2
